TPU v7x, 512 devices: a whole 4x4x16 slice. The times are simulated.
512 devices in a mesh: dp: 8 (over z_lo, core), gx: 4 (over x), gy: 4 (over z_hi), gz: 4 (over y).
Axes of the slice: x: 4, y: 4, z: 16 (z_hi: 4, z_lo: 4; z = z_hi * 4 + z_lo), core: 2. Of those that a mesh axis runs over, the one named last changes fastest.
Arguments:
- activations: bfloat16 [8192, 8192], P(('dp', 'gy'), 'gx'), may hold values from -0.06591797 to 0.06591797
- out_grad: bfloat16 [8192, 8192], P(('dp', 'gy'), ('gz', 'gx')), may hold values from -6 to 6
- weight: bfloat16 [8192, 8192], P(('gx', 'gy'), 'gz'), may hold values from -0.09375 to 0.09375
Outputs:
- input_grad: bfloat16 [8192, 8192], P(('dp', 'gy'), ('gx', 'gz'))
- weight_grad: float32 [8192, 8192], P(('gx', 'dp'), ('gz', 'gy'))
All inputs are finite; a program needn't handle non-finite values.
Results may differ from a plain program's by a relative error of at most 0.015.
Values may be sent and summed in bfloat16 or wider, within the bound.
No kernel may reach another device: no remote copies, remote signals or barrier semaphores. Data moves between devices by JAX's collectives and lax.ppermute only.
A program may use at most 64 MiB of HBM per device.

v0:
```python
import jax
import jax.numpy as jnp
from jax import lax
from jax.sharding import PartitionSpec as P


def body(activations, out_grad, weight):
    grad_rows = lax.all_gather(out_grad, "gx", axis=1, tiled=True)
    input_all, grad_all = (
        lax.all_gather(activations, "gy", axis=0, tiled=True),
        lax.all_gather(grad_rows, "gy", axis=0, tiled=True),
    )
    partial_terms = lax.dot_general(
        grad_rows,
        lax.all_gather(weight, "gy", axis=0, tiled=True),
        (((1,), (1,)), ((), ())),
        preferred_element_type=jnp.float32,
    )
    input_grad = lax.psum_scatter(
        partial_terms.astype(jnp.bfloat16), "gz", scatter_dimension=1, tiled=True
    )
    span = grad_all.shape[1] // lax.axis_size("gy")
    columns = lax.dynamic_slice_in_dim(grad_all, lax.axis_index("gy") * span, span, 1)
    share = lax.dot_general(
        input_all, columns, (((0,), (0,)), ((), ())), preferred_element_type=jnp.float32
    )
    weight_grad = lax.psum_scatter(
        share.astype(jnp.bfloat16), "dp", scatter_dimension=0, tiled=True
    ).astype(jnp.float32)
    return (input_grad, weight_grad)


def solution(mesh):
    return jax.shard_map(
        body,
        mesh=mesh,
        in_specs=(P(("dp", "gy"), "gx"), P(("dp", "gy"), ("gz", "gx")), P(("gx", "gy"), "gz")),
        out_specs=(P(("dp", "gy"), ("gx", "gz")), P(("gx", "dp"), ("gz", "gy"))),
        check_vma=False,
    )
```

profile of v0, /device:TPU:6, one launch (start us, length us, event | category | flops | bytes accessed | tf_op | source)
XLA Modules:
  0.0 759.9 jit_solution(8080950362944951511)
XLA Ops:
  7.2 0.0 all-gather.5.cloned.1.call-start
  7.2 0.7 all-gather.5.cloned.1.call-update
  7.9 0.0 all-gather.11.cloned.1.call-start
  7.9 0.7 all-gather.11.cloned.1.call-update
  8.6 0.0 all-gather.9.cloned.1.call-start
  8.7 36.6 %all-gather.5.cloned.1.call-done = bf16[256,2048]{1,0:T(8,128)(2,1)} async-done(((bf16[256,512]{1,0:T(8,128)(2,1)}), bf16[256,2048]{1,0:T(8,128)(2,1)}) %all-gather.5.cloned.1.call-update) | async-done | bytes 1048592 | tf_op jit(solution)/shard_map/all_gather | solution.py:8
  45.2 0.0 all-gather.9.cloned.1.call-update
  45.3 0.0 all-gather.7.cloned.1.call-start
  45.3 0.5 all-gather.7.cloned.1.call-update
  45.8 0.0 reduce-scatter.5.cloned.1.call-start
  45.9 0.0 copy-start
  45.9 165.7 %all-gather.11.cloned.1.call-done = bf16[1024,2048]{1,0:T(8,128)(2,1)} async-done(((bf16[256,2048]{1,0:T(8,128)(2,1)}), bf16[1024,2048]{1,0:T(8,128)(2,1)}) %all-gather.11.cloned.1.call-update) | async-done | bytes 4194320 | tf_op jit(solution)/shard_map/all_gather | solution.py:10
  211.6 161.6 %all-gather.9.cloned.1.call-done = bf16[1024,2048]{1,0:T(8,128)(2,1)} async-done(((bf16[256,2048]{1,0:T(8,128)(2,1)}), bf16[1024,2048]{1,0:T(8,128)(2,1)}) %all-gather.9.cloned.1.call-update) | async-done | bytes 4194320 | tf_op jit(solution)/shard_map/all_gather | solution.py:11
  373.2 6.2 fusion
  379.4 0.0 reduce-scatter.5.cloned.1.call-update
  379.4 0.0 reduce-scatter.3.cloned.1.call-start
  379.5 291.4 %all-gather.7.cloned.1.call-done = bf16[2048,2048]{1,0:T(8,128)(2,1)} async-done(((bf16[512,2048]{1,0:T(8,128)(2,1)}), bf16[2048,2048]{1,0:T(8,128)(2,1)}) %all-gather.7.cloned.1.call-update) | async-done | bytes 8388624 | tf_op jit(solution)/shard_map/all_gather | solution.py:15
  670.9 0.0 copy-done
  670.9 6.8 convolution_convert_fusion.1
  677.7 0.0 reduce-scatter.3.cloned.1.call-update
  677.7 41.8 %reduce-scatter.5.cloned.1.call-done = bf16[256,512]{0,1:T(8,128)(2,1)} async-done(((bf16[2048,512]{0,1:T(8,128)(2,1)}), bf16[256,512]{0,1:T(8,128)(2,1)}) %reduce-scatter.5.cloned.1.call-update) | async-done | bytes 262160 | tf_op jit(solution)/shard_map/reduce_scatter | solution.py:27
  719.6 1.9 copy.5
  721.4 31.6 %reduce-scatter.3.cloned.1.call-done = bf16[256,512]{1,0:T(8,128)(2,1)} async-done(((bf16[256,2048]{1,0:T(8,128)(2,1)}), bf16[256,512]{1,0:T(8,128)(2,1)}) %reduce-scatter.3.cloned.1.call-update) | async-done | bytes 262160 | tf_op jit(solution)/shard_map/reduce_scatter | solution.py:19
Async XLA Ops:
  7.2 38.1 %all-gather.5.cloned.1.call-start = ((), (), s32[]{:S(2)}) async-start(), calls=%async_computation.2 | async-start | bytes 1310720 | tf_op jit(solution)/shard_map/all_gather | solution.py:8
  7.9 203.7 %all-gather.11.cloned.1.call-start = ((), (), s32[]{:S(2)}) async-start(), calls=%async_computation.6 | async-start | bytes 5242880 | tf_op jit(solution)/shard_map/all_gather | solution.py:10
  8.6 364.5 %all-gather.9.cloned.1.call-start = ((), (), s32[]{:S(2)}) async-start(), calls=%async_computation.5 | async-start | bytes 5242880 | tf_op jit(solution)/shard_map/all_gather | solution.py:11
  45.3 625.6 %all-gather.7.cloned.1.call-start = ((), (), s32[]{:S(2)}) async-start(), calls=%async_computation.3 | async-start | bytes 10485760 | tf_op jit(solution)/shard_map/all_gather | solution.py:15
  45.8 673.7 %reduce-scatter.5.cloned.1.call-start = ((), (), s32[]{:S(2)}) async-start(), calls=%async_computation.7 | async-start | bytes 2359296 | tf_op jit(solution)/shard_map/reduce_scatter | solution.py:27
  45.9 625.0 %copy-start = (bf16[256,2048]{1,0:T(8,128)(2,1)S(1)}, bf16[256,2048]{1,0:T(8,128)(2,1)}, u32[]{:S(2)}) copy-start(bf16[256,2048]{1,0:T(8,128)(2,1)} %all-gather.5.cloned.1.call-done) | copy-start | bytes 3145732
  379.4 373.7 %reduce-scatter.3.cloned.1.call-start = ((), (), s32[]{:S(2)}) async-start(), calls=%async_computation.4 | async-start | bytes 1310720 | tf_op jit(solution)/shard_map/reduce_scatter | solution.py:19
Sparse Core Ops, SparseCore 0:
  10.1 35.1 all-gather.4
  47.3 164.2 all-gather.10
  213.7 159.4 all-gather.8
  375.1 295.6 all-gather.6
  673.6 45.9 reduce-scatter.4
  722.8 30.2 reduce-scatter.2
where the time goes:
time: 760 us
  waiting for transfers between devices  731 us (96%)
  between operations  14.1 us (2%)
  matrix products  13 us (2%)
    all_gather x1, waiting for transfers between devices, body(): lax.all_gather(weight, 'gy', axis=0, tiled=True)  291 us
    all_gather x1, waiting for transfers between devices, body(): lax.all_gather(activations, 'gy', axis=0, tiled=True)  166 us
    all_gather x1, waiting for transfers between devices, body(): lax.all_gather(grad_rows, 'gy', axis=0, tiled=True)  162 us
    reduce_scatter x1, waiting for transfers between devices, body(): lax.psum_scatter(share.astype(jnp.bfloat16), 'dp', scatter_dimension=0, t...  41.8 us
    all_gather x1, waiting for transfers between devices, body(): grad_rows = lax.all_gather(out_grad, 'gx', axis=1, tiled=True)  36.6 us
    reduce_scatter x1, waiting for transfers between devices, body(): lax.psum_scatter(partial_terms.astype(jnp.bfloat16), 'gz', scatter_dimens...  31.6 us
  transfers between devices with their start and end apart: 6, of which 6 were waited for; matrix products, arithmetic and copies ran while one was open for 2% of the time, Pallas kernels for 0%

commit v1 on v0

v1 whole, which is shorter than its diff:
```python
import jax
import jax.numpy as jnp
from jax import lax
from jax.sharding import PartitionSpec as P

BF16, F32 = jnp.bfloat16, jnp.float32


def exchange(x, axis, groups=None):
    return lax.all_to_all(x, axis, 0, 0, tiled=True, axis_index_groups=groups)


def gather(x, axis):
    n = lax.axis_size(axis)
    return exchange(jnp.broadcast_to(x[None], (n,) + x.shape), axis)


def total(parts):
    return jnp.sum(parts.astype(F32), axis=0)


def body(a, g, w):
    n = lax.axis_size("gy")
    rows, span = g.shape
    sub = rows // n
    g_all = gather(gather(g, "gy").reshape(n * rows, span), "gx")
    mine = lax.dynamic_slice_in_dim(a, lax.axis_index("gz") * sub, sub, 0)
    got = exchange(mine.reshape(sub, n, span).transpose(1, 0, 2), "gy")
    a_q = gather(got, "gz").transpose(1, 0, 2, 3).reshape(n * rows, span)
    part = lax.dot_general(
        g_all, w.reshape(span, n, span), (((0, 2), (1, 2)), ((), ())), preferred_element_type=F32
    )
    part = part.astype(BF16).reshape(n, n, sub, span).transpose(1, 0, 2, 3)
    dx = total(exchange(part, "gz")).astype(BF16)
    dx = exchange(dx, "gy")
    dx = exchange(dx, "gz").reshape(rows, span)
    share = lax.dot_general(g_all, a_q, (((1,), (0,)), ((), ())), preferred_element_type=F32)
    share = share.astype(BF16).transpose(0, 2, 1).reshape(n, 2, rows, span)
    core = lax.axis_index("dp") % 2
    keep = lax.dynamic_index_in_dim(share, core, 1, keepdims=False)
    send = lax.dynamic_index_in_dim(share, 1 - core, 1, keepdims=False)
    other = lax.ppermute(send, "dp", [(i, i ^ 1) for i in range(8)])
    both = (keep.astype(F32) + other.astype(F32)).astype(BF16)
    dw = total(exchange(both, "dp", [[0, 2, 4, 6], [1, 3, 5, 7]])).astype(BF16)
    swap = [
        ((lo * 2 + c) * 4 + hi, (hi * 2 + c) * 4 + lo)
        for lo in range(4) for c in range(2) for hi in range(4)
    ]
    dw = lax.ppermute(dw, ("dp", "gy"), swap).astype(F32)
    return dx, dw


def solution(mesh):
    return jax.shard_map(
        body,
        mesh=mesh,
        in_specs=(P(("dp", "gy"), "gx"), P(("dp", "gy"), ("gz", "gx")), P(("gx", "gy"), "gz")),
        out_specs=(P(("dp", "gy"), ("gx", "gz")), P(("gx", "dp"), ("gz", "gy"))),
        check_vma=False,
    )
```

time: 760 us -> 263 us (0.35)
  the two profiles are of different devices: /device:TPU:6 before, /device:TPU:65 now
where the time goes in v1:
time: 263 us; the launch traced here: 262 us
  blocking collectives  112 us (43%)
  waiting for transfers between devices  96.9 us (37%)
  starting transfers between devices  31.7 us (12%)
  matrix products  9.12 us (3%)
  local copies, waits for them, and re-layouts  7.15 us (3%)
  other arithmetic  4.87 us (2%)
    all_to_all x4, blocking collectives, exchange(): return lax.all_to_all(x, axis, 0, 0, tiled=True, axis_index_groups=groups)  112 us
    all_to_all x4, waiting for transfers between devices, exchange(): return lax.all_to_all(x, axis, 0, 0, tiled=True, axis_index_groups=groups)  84.4 us
    all_to_all x4, starting transfers between devices, exchange(): return lax.all_to_all(x, axis, 0, 0, tiled=True, axis_index_groups=groups)  15.4 us
    ppermute x1, starting transfers between devices, body(): dw = lax.ppermute(dw, ('dp', 'gy'), swap).astype(F32)  13 us
    ppermute x1, waiting for transfers between devices, body(): dw = lax.ppermute(dw, ('dp', 'gy'), swap).astype(F32)  12.5 us
  transfers between devices with their start and end apart: 6, of which 5 were waited for; matrix products, arithmetic and copies ran while one was open for 4% of the time, Pallas kernels for 0%

profile of v1, /device:TPU:65, one launch (start us, length us, event | category | flops | bytes accessed | tf_op | source)
XLA Modules:
  0.0 262.1 jit_solution(16466572299994227369)
XLA Ops:
  0.6 0.0 copy-start
  0.6 1.2 copy-done
  1.9 0.2 reshape.30
  2.1 0.0 copy-start.2
  2.1 33.7 %all_to_all.40 = bf16[4,64,512]{2,1,0:T(8,128)(2,1)S(1)} all-to-all(bf16[4,64,512]{2,1,0:T(8,128)(2,1)S(1)} %copy.11), channel_id=1, replica_groups=mesh['dp'=8,'gx'=4,'gy'=4,'gz'=4] {'gy'}, dimensions={0} | all-to-all | bytes 524288 | tf_op jit(solution)/shard_map/all_to_all | solution.py:10
  35.8 0.1 broadcast_in_dim.22
  35.9 17.3 %all_to_all.41 = bf16[4,4,64,512]{3,2,1,0:T(8,128)(2,1)S(1)} all-to-all(bf16[4,4,64,512]{3,2,1,0:T(8,128)(2,1)S(1)} %broadcast_in_dim.22), channel_id=1, replica_groups=mesh['dp'=8,'gx'=4,'gy'=4,'gz'=4] {'gz'}, dimensions={0} | all-to-all | bytes 2097152 | tf_op jit(solution)/shard_map/all_to_all | solution.py:10
  53.2 0.0 copy-done.2
  53.2 0.1 broadcast_in_dim.8
  53.3 52.7 %all_to_all.42 = bf16[4,256,512]{2,1,0:T(8,128)(2,1)S(1)} all-to-all(bf16[4,256,512]{2,1,0:T(8,128)(2,1)S(1)} %broadcast_in_dim.8), channel_id=1, replica_groups=mesh['dp'=8,'gx'=4,'gy'=4,'gz'=4] {'gy'}, dimensions={0} | all-to-all | bytes 2097152 | tf_op jit(solution)/shard_map/all_to_all | solution.py:10
  106.0 2.3 broadcast_in_dim.10
  108.3 4.8 %all-to-all-start.1 = ((bf16[4,1024,512]{2,1,0:T(8,128)(2,1)}), bf16[4,1024,512]{2,1,0:T(8,128)(2,1)}, u32[]{:S(2)}, u32[]{:S(2)}) async-start(bf16[4,1024,512]{2,1,0:T(8,128)(2,1)} %broadcast_in_dim.10), calls=%async_computation.1 | async-start | bytes 8388608 | tf_op jit(solution)/shard_map/all_to_all | solution.py:10
  113.2 0.1 copy.12
  113.3 48.3 %all-to-all-done.1 = bf16[4,1024,512]{2,1,0:T(8,128)(2,1)} async-done(((bf16[4,1024,512]{2,1,0:T(8,128)(2,1)}), bf16[4,1024,512]{2,1,0:T(8,128)(2,1)}, u32[]{:S(2)}, u32[]{:S(2)}) %all-to-all-start.1) | async-done | bytes 4194336 | tf_op jit(solution)/shard_map/all_to_all | solution.py:10
  161.5 4.6 %convolution_convert_fusion = bf16[512,4,512]{2,0,1:T(8,128)(2,1)S(1)} fusion(bf16[1024,512,1]{1,0,2:T(8,128)(2,1)S(1)} %bitcast.34, bf16[4,1024,512]{2,1,0:T(8,128)(2,1)} %all-to-all-done.1), kind=kOutput, calls=%fused_computation.6 | convolution fusion | flops 2148532224 | bytes 7340032 | tf_op jit(solution)/shard_map/dot_general | solution.py:37
  166.1 0.0 copy-start.1
  166.1 0.0 copy-start.3
  166.1 1.3 copy-done.1
  167.4 0.1 dynamic-slice_bitcast_fusion
  167.5 3.4 %collective-permute-start = (bf16[4,256,512]{2,1,0:T(8,128)(2,1)S(1)}, bf16[4,256,512]{2,1,0:T(8,128)(2,1)}, u32[]{:S(2)}, u32[]{:S(2)}) collective-permute-start(bf16[4,256,512]{2,1,0:T(8,128)(2,1)S(1)} %dynamic-slice_bitcast_fusion), channel_id=1, source_target_pairs={{0,64},{64,0},{128,192},{192,128},{256,320},{320,256},{384,448},{4... | collective-permute-start | bytes 3145736 | tf_op jit(solution)/shard_map/ppermute | solution.py:42
  170.9 0.0 copy-done.3
  170.9 4.6 %bitcast_convert_fusion = bf16[1024,512]{1,0:T(8,128)(2,1)S(1)} fusion(bf16[4,1024,512]{2,1,0:T(8,128)(2,1)} %all-to-all-done.1, bf16[64,4,8,512]{3,2,1,0:T(8,128)(2,1)S(1)} %bitcast.38), kind=kOutput, calls=%fused_computation.5 | convolution fusion | flops 2148007936 | bytes 7340032 | tf_op jit(solution)/shard_map/dot_general | solution.py:30
  175.4 1.0 copy.24
  176.5 3.5 %all-to-all-start.2 = ((bf16[4,4,64,512]{3,2,1,0:T(8,128)(2,1)}), bf16[4,4,64,512]{3,2,1,0:T(8,128)(2,1)S(1)}, u32[]{:S(2)}, u32[]{:S(2)}) async-start(bf16[4,4,64,512]{3,2,1,0:T(8,128)(2,1)} %bitcast.30), calls=%async_computation.2 | async-start | bytes 2097152 | tf_op jit(solution)/shard_map/all_to_all | solution.py:10
  180.0 0.0 collective-permute-done
  180.0 2.9 %fusion.3 = bf16[4,256,512]{2,1,0:T(8,128)(2,1)} fusion(bf16[4,256,512]{2,1,0:T(8,128)(2,1)} %collective-permute-done, bf16[4,2,256,512]{3,2,1,0:T(8,128)(2,1)} %bitcast.33, s32[]{:T(128)S(6)} %select_n.19), kind=kLoop, calls=%fused_computation.4 | loop fusion | flops 2097152 | bytes 3145732 | tf_op jit(solution)/shard_map/convert_element_type | solution.py:43
  182.9 12.3 %all-to-all-done.2 = bf16[4,4,64,512]{3,2,1,0:T(8,128)(2,1)S(1)} async-done(((bf16[4,4,64,512]{3,2,1,0:T(8,128)(2,1)}), bf16[4,4,64,512]{3,2,1,0:T(8,128)(2,1)S(1)}, u32[]{:S(2)}, u32[]{:S(2)}) %all-to-all-start.2) | async-done | bytes 1048608 | tf_op jit(solution)/shard_map/all_to_all | solution.py:10
  195.2 3.6 %all-to-all-start.7 = ((bf16[4,256,512]{2,1,0:T(8,128)(2,1)}), bf16[4,256,512]{2,1,0:T(8,128)(2,1)S(1)}, u32[]{:S(2)}, u32[]{:S(2)}) async-start(bf16[4,256,512]{2,1,0:T(8,128)(2,1)} %fusion.3), calls=%async_computation.7 | async-start | bytes 2097152 | tf_op jit(solution)/shard_map/all_to_all | solution.py:10
  198.9 0.9 reduce_sum.24
  199.8 21.3 %all-to-all-done.7 = bf16[4,256,512]{2,1,0:T(8,128)(2,1)S(1)} async-done(((bf16[4,256,512]{2,1,0:T(8,128)(2,1)}), bf16[4,256,512]{2,1,0:T(8,128)(2,1)S(1)}, u32[]{:S(2)}, u32[]{:S(2)}) %all-to-all-start.7) | async-done | bytes 1048608 | tf_op jit(solution)/shard_map/all_to_all | solution.py:10
  221.1 3.4 %all-to-all-start.3 = ((bf16[4,64,512]{2,1,0:T(8,128)(2,1)}), bf16[4,64,512]{2,1,0:T(8,128)(2,1)S(1)}, u32[]{:S(2)}, u32[]{:S(2)}) async-start(bf16[4,64,512]{2,1,0:T(8,128)(2,1)} %reduce_sum.24), calls=%async_computation.3 | async-start | bytes 524288 | tf_op jit(solution)/shard_map/all_to_all | solution.py:10
  224.5 0.2 reduce_sum.25
  224.7 13.0 %collective-permute-start.1 = (bf16[256,512]{1,0:T(8,128)(2,1)S(1)}, bf16[256,512]{1,0:T(8,128)(2,1)S(1)}, u32[]{:S(2)}, u32[]{:S(2)}) collective-permute-start(bf16[256,512]{1,0:T(8,128)(2,1)S(1)} %reduce_sum.25), channel_id=1, source_target_pairs={{0,0},{4,128},{8,256},{12,384},{64,64},{68,192},{72,320},{76,448},... | collective-permute-start | bytes 786440 | tf_op jit(solution)/shard_map/ppermute | solution.py:49
  237.7 2.4 all-to-all-done.3
  240.2 7.9 %all_to_all.43 = bf16[4,64,512]{2,1,0:T(8,128)(2,1)S(1)} all-to-all(bf16[4,64,512]{2,1,0:T(8,128)(2,1)S(1)} %all-to-all-done.3), channel_id=1, replica_groups=mesh['dp'=8,'gx'=4,'gy'=4,'gz'=4] {'gz'}, dimensions={0} | all-to-all | bytes 524288 | tf_op jit(solution)/shard_map/all_to_all | solution.py:10
  248.1 12.5 %collective-permute-done.1 = bf16[256,512]{1,0:T(8,128)(2,1)S(1)} collective-permute-done((bf16[256,512]{1,0:T(8,128)(2,1)S(1)}, bf16[256,512]{1,0:T(8,128)(2,1)S(1)}, u32[]{:S(2)}, u32[]{:S(2)}) %collective-permute-start.1) | collective-permute-done | bytes 262176 | tf_op jit(solution)/shard_map/ppermute | solution.py:49
  260.6 0.9 convert_element_type.36
  261.4 0.7 copy.26
  (2 shorter events, 0.1 us)
Async XLA Ops:
  0.6 1.2 copy-start
  2.1 51.1 %copy-start.2 = (bf16[256,512]{1,0:T(8,128)(2,1)S(1)}, bf16[256,512]{1,0:T(8,128)(2,1)}, u32[]{:S(2)}) copy-start(bf16[256,512]{1,0:T(8,128)(2,1)} %param.4) | copy-start | bytes 786436
  108.3 53.2 %all-to-all-start.1 = ((bf16[4,1024,512]{2,1,0:T(8,128)(2,1)}), bf16[4,1024,512]{2,1,0:T(8,128)(2,1)}, u32[]{:S(2)}, u32[]{:S(2)}) async-start(bf16[4,1024,512]{2,1,0:T(8,128)(2,1)} %broadcast_in_dim.10), calls=%async_computation.1 | async-start | bytes 8388608 | tf_op jit(solution)/shard_map/all_to_all | solution.py:10
  166.1 1.3 copy-start.1
  166.1 4.8 %copy-start.3 = (bf16[512,2048]{1,0:T(8,128)(2,1)S(1)}, bf16[512,2048]{1,0:T(8,128)(2,1)}, u32[]{:S(2)}) copy-start(bf16[512,2048]{1,0:T(8,128)(2,1)} %param.5) | copy-start | bytes 6291460
  167.5 12.5 %collective-permute-start = (bf16[4,256,512]{2,1,0:T(8,128)(2,1)S(1)}, bf16[4,256,512]{2,1,0:T(8,128)(2,1)}, u32[]{:S(2)}, u32[]{:S(2)}) collective-permute-start(bf16[4,256,512]{2,1,0:T(8,128)(2,1)S(1)} %dynamic-slice_bitcast_fusion), channel_id=1, source_target_pairs={{0,64},{64,0},{128,192},{192,128},{256,320},{320,256},{384,448},{4... | collective-permute-start | bytes 3145736 | tf_op jit(solution)/shard_map/ppermute | solution.py:42
  176.5 18.7 %all-to-all-start.2 = ((bf16[4,4,64,512]{3,2,1,0:T(8,128)(2,1)}), bf16[4,4,64,512]{3,2,1,0:T(8,128)(2,1)S(1)}, u32[]{:S(2)}, u32[]{:S(2)}) async-start(bf16[4,4,64,512]{3,2,1,0:T(8,128)(2,1)} %bitcast.30), calls=%async_computation.2 | async-start | bytes 2097152 | tf_op jit(solution)/shard_map/all_to_all | solution.py:10
  195.2 25.9 %all-to-all-start.7 = ((bf16[4,256,512]{2,1,0:T(8,128)(2,1)}), bf16[4,256,512]{2,1,0:T(8,128)(2,1)S(1)}, u32[]{:S(2)}, u32[]{:S(2)}) async-start(bf16[4,256,512]{2,1,0:T(8,128)(2,1)} %fusion.3), calls=%async_computation.7 | async-start | bytes 2097152 | tf_op jit(solution)/shard_map/all_to_all | solution.py:10
  221.1 19.1 %all-to-all-start.3 = ((bf16[4,64,512]{2,1,0:T(8,128)(2,1)}), bf16[4,64,512]{2,1,0:T(8,128)(2,1)S(1)}, u32[]{:S(2)}, u32[]{:S(2)}) async-start(bf16[4,64,512]{2,1,0:T(8,128)(2,1)} %reduce_sum.24), calls=%async_computation.3 | async-start | bytes 524288 | tf_op jit(solution)/shard_map/all_to_all | solution.py:10
  224.7 35.8 %collective-permute-start.1 = (bf16[256,512]{1,0:T(8,128)(2,1)S(1)}, bf16[256,512]{1,0:T(8,128)(2,1)S(1)}, u32[]{:S(2)}, u32[]{:S(2)}) collective-permute-start(bf16[256,512]{1,0:T(8,128)(2,1)S(1)} %reduce_sum.25), channel_id=1, source_target_pairs={{0,0},{4,128},{8,256},{12,384},{64,64},{68,192},{72,320},{76,448},... | collective-permute-start | bytes 786440 | tf_op jit(solution)/shard_map/ppermute | solution.py:49

commit v2 on v1

v2 whole, which is shorter than its diff:
```python
import jax
import jax.numpy as jnp
from jax import lax
from jax.experimental import pallas as pl
from jax.experimental.pallas import tpu as pltpu
from jax.sharding import PartitionSpec as P

BF16, F32 = jnp.bfloat16, jnp.float32


def exchange(x, axis):
    return lax.all_to_all(x, axis, 0, 0, tiled=True)


def gather(x, axis):
    n = lax.axis_size(axis)
    return exchange(jnp.broadcast_to(x[None], (n,) + x.shape), axis)


def shift(x, axis, s):
    n = lax.axis_size(axis)
    return lax.ppermute(x, axis, [(i, (i + s) % n) for i in range(n)])


def after(x, *others):
    return pl.pallas_call(
        lambda *refs: None,
        out_shape=jax.ShapeDtypeStruct(x.shape, x.dtype),
        in_specs=[pl.BlockSpec(memory_space=pl.ANY)] * (1 + len(others)),
        out_specs=pl.BlockSpec(memory_space=pl.ANY),
        input_output_aliases={0: 0},
        name="after",
    )(x, *others)


def block(x, i, size, axis):
    return lax.dynamic_slice_in_dim(x, i * size, size, axis)


def turned(parts, first):
    n = len(parts)
    return lax.dynamic_slice_in_dim(jnp.stack(parts * 2), first, n, 0)


def body(a, g, w):
    n = lax.axis_size("gy")
    me, gz = lax.axis_index("gy"), lax.axis_index("gz")
    rows, span = g.shape
    sub, half = rows // n, rows // 2
    w = w.reshape(span, n, span)
    mine = block(a, gz, sub, 0)

    def piece(s):
        return block(mine, lax.rem(me + s, n), span, 1)

    far = piece(2)
    up = shift(jnp.concatenate([g, piece(1), far[: sub // 2]], 0), "gy", 1)
    down = shift(jnp.concatenate([g[half:], g[:half], piece(3), far[sub // 2 :]], 0), "gy", 3)
    b0 = gather(g, "gx")
    via_up = jnp.concatenate([up[:half], up[rows + sub :]], 0)
    via_down = jnp.concatenate([down[:half], down[rows + sub :]], 0)
    far = [shift(after(via_up, b0), "gy", 1), shift(after(via_down, b0), "gy", 3)]
    b13 = gather(jnp.concatenate([up[:rows], down[half:rows], down[:half]], 0), "gx")
    b2 = gather(after(jnp.concatenate([t[:half] for t in far], 0), b13), "gx")
    x = [up[rows : rows + sub], down[rows : rows + sub], jnp.concatenate([t[half:] for t in far], 0)]
    x = jnp.stack(x)
    x = [x] + [shift(x, "gz", s) for s in (1, 2, 3)]
    x = turned([x[0], x[3], x[2], x[1]], lax.rem(n - gz, n))
    acts = x.transpose(1, 0, 2, 3).reshape(3 * rows, span)
    blocks = [b0, b13, b2]
    terms = [
        lax.dot_general(t, w, (((0, 2), (1, 2)), ((), ())), preferred_element_type=F32).astype(BF16) for t in blocks
    ]
    terms = jnp.concatenate(terms, 0).reshape(n, n, sub, span).transpose(1, 0, 2, 3)
    dx = jnp.sum(exchange(terms, "gz").astype(F32), axis=0).astype(BF16)
    dx = turned([dx[0], dx[2], dx[3], dx[1]], lax.rem(n - me, n))
    dx = exchange(exchange(dx, "gy"), "gz").reshape(rows, span)
    acts = [block(a, me, span, 1), acts[: 2 * rows], acts[2 * rows :]]
    dp = lax.axis_index("dp")
    core, lo = lax.rem(dp, 2), lax.div(dp, 2)

    def share(i):
        out = sum(
            lax.dot_general(block(x, i, rows, 1), t, (((0,), (1,)), ((), ())), preferred_element_type=F32)
            for x, t in zip(acts, blocks)
        )
        return out.transpose(1, 0, 2).astype(BF16)

    def partner(x, bit):
        return lax.ppermute(x, "dp", [(i, i ^ bit) for i in range(8)])

    def added(x, y):
        return (x.astype(F32) + y.astype(F32)).astype(BF16)

    other = partner(share(1 - core), 1)
    dw = added(share(core), other).reshape(2, 2, rows, span)
    low, high = lax.rem(lo, 2), lax.div(lo, 2)
    dw = added(block(dw, low, 1, 1), partner(block(dw, 1 - low, 1, 1), 2))[:, 0]
    dw = added(block(dw, high, 1, 0), partner(block(dw, 1 - high, 1, 0), 4))[0]
    swap = [
        ((lo * 2 + c) * 4 + hi, (hi * 2 + c) * 4 + lo)
        for lo in range(4) for c in range(2) for hi in range(4)
    ]
    dw = lax.ppermute(dw, ("dp", "gy"), swap).astype(F32)
    return dx, dw


def solution(mesh):
    return jax.shard_map(
        body,
        mesh=mesh,
        in_specs=(P(("dp", "gy"), "gx"), P(("dp", "gy"), ("gz", "gx")), P(("gx", "gy"), "gz")),
        out_specs=(P(("dp", "gy"), ("gx", "gz")), P(("gx", "dp"), ("gz", "gy"))),
        check_vma=False,
    )
```

time: 263 us -> 211 us (0.80)
  blocking collectives: 112 us -> 7.92 us
  starting transfers between devices: 31.7 us -> 70.2 us
  waiting for transfers between devices: 96.9 us -> 82.2 us
  matrix products: 9.12 us -> 21.7 us
  local copies, waits for them, and re-layouts: 7.15 us -> 19.6 us
    all_to_all x4 -> x1, blocking collectives: 112 us -> 7.92 us  [exchange(): return lax.all_to_all(x, axis, 0, 0, tiled=True)]
    all_to_all x4 -> x5, waiting for transfers between devices: 84.4 us -> 8.76 us  [exchange(): return lax.all_to_all(x, axis, 0, 0, tiled=True)]
    ppermute x1 -> x10, waiting for transfers between devices: 0.01 us -> 60.9 us  [the longest x7 34.1 us: shift(): return lax.ppermute(x, axis, [(i, (i + s) % n) for i in range(n)])]
    ppermute x1 -> x10, starting transfers between devices: 3.36 us -> 48.2 us  [the longest x7 31.4 us: shift(): return lax.ppermute(x, axis, [(i, (i + s) % n) for i in range(n)])]
    dot_general x2 -> x9, matrix products: 9.12 us -> 21.7 us  [the longest x6 14.1 us: share(): lax.dot_general(block(x, i, rows, 1), t, (((0,), (1,)), ((), ())), prefer...]
    ppermute x1, starting transfers between devices: 13 us -> 1.92 us  [body(): dw = lax.ppermute(dw, ('dp', 'gy'), swap).astype(F32)]
    all_to_all x4 -> x5, starting transfers between devices: 15.4 us -> 20 us  [exchange(): return lax.all_to_all(x, axis, 0, 0, tiled=True)]
    slice x0 -> x14, local copies, waits for them, and re-layouts: none -> 3.89 us  [the longest x1 1.02 us: body(): g[half:]]
  transfers between devices with their start and end apart: 6 -> 16, of which waited for: 5 -> 10; matrix products, arithmetic and copies ran while one was open for 4% -> 15% of each run, Pallas kernels for 0% -> 0%
where the time goes in v2:
time: 211 us; the launch traced here: 210 us
  waiting for transfers between devices  82.2 us (39%)
  starting transfers between devices  70.2 us (33%)
  matrix products  21.7 us (10%)
  local copies, waits for them, and re-layouts  19.6 us (9%)
  blocking collectives  7.92 us (4%)
  other arithmetic  7.11 us (3%)
    ppermute x7, waiting for transfers between devices, shift(): return lax.ppermute(x, axis, [(i, (i + s) % n) for i in range(n)])  34.1 us
    ppermute x7, starting transfers between devices, shift(): return lax.ppermute(x, axis, [(i, (i + s) % n) for i in range(n)])  31.4 us
    ppermute x3, waiting for transfers between devices, partner(): return lax.ppermute(x, 'dp', [(i, i ^ bit) for i in range(8)])  26.7 us
    all_to_all x5, starting transfers between devices, exchange(): return lax.all_to_all(x, axis, 0, 0, tiled=True)  20 us
    ppermute x3, starting transfers between devices, partner(): return lax.ppermute(x, 'dp', [(i, i ^ bit) for i in range(8)])  16.8 us
    dot_general x6, matrix products, share(): lax.dot_general(block(x, i, rows, 1), t, (((0,), (1,)), ((), ())), prefer...  14.1 us
    ppermute x1, waiting for transfers between devices, body(): dw = lax.ppermute(dw, ('dp', 'gy'), swap).astype(F32)  12.6 us
    all_to_all x5, waiting for transfers between devices, exchange(): return lax.all_to_all(x, axis, 0, 0, tiled=True)  8.76 us
  transfers between devices with their start and end apart: 16, of which 10 were waited for; matrix products, arithmetic and copies ran while one was open for 15% of the time, Pallas kernels for 0%

profile of v2, /device:TPU:65, one launch (start us, length us, event | category | flops | bytes accessed | tf_op | source)
XLA Modules:
  0.0 209.9 jit_solution(6036480640521278659)
XLA Ops:
  0.7 1.0 fusion.56
  1.7 1.0 fusion.54
  2.7 1.1 fusion.53
  3.8 10.7 %collective-permute-start.1 = (bf16[352,512]{1,0:T(8,128)(2,1)S(1)}, bf16[352,512]{1,0:T(8,128)(2,1)S(1)}, u32[]{:S(2)}, u32[]{:S(2)}) collective-permute-start(bf16[352,512]{1,0:T(8,128)(2,1)S(1)} %pad_maximum_fusion.3), channel_id=1, source_target_pairs={{0,12},{4,0},{8,4},{12,8},{1,13},{5,1},{9,5},{13,9},{2,14},{6,2},{... | collective-permute-start | bytes 1081352 | tf_op jit(solution)/shard_map/ppermute | solution.py:22
  14.5 1.0 pad_maximum_fusion.2
  15.5 1.9 collective-permute-start
  17.4 1.1 broadcast_in_dim.6
  18.5 4.0 %all-to-all-start = ((bf16[4,256,512]{2,1,0:T(8,128)(2,1)}), bf16[4,256,512]{2,1,0:T(8,128)(2,1)S(1)}, u32[]{:S(2)}, u32[]{:S(2)}) async-start(bf16[4,256,512]{2,1,0:T(8,128)(2,1)} %broadcast_in_dim.6), calls=%async_computation | async-start | bytes 2097152 | tf_op jit(solution)/shard_map/all_to_all | solution.py:12
  22.5 14.0 %collective-permute-done.1 = bf16[352,512]{1,0:T(8,128)(2,1)S(1)} collective-permute-done((bf16[352,512]{1,0:T(8,128)(2,1)S(1)}, bf16[352,512]{1,0:T(8,128)(2,1)S(1)}, u32[]{:S(2)}, u32[]{:S(2)}) %collective-permute-start.1) | collective-permute-done | bytes 360480 | tf_op jit(solution)/shard_map/ppermute | solution.py:22
  36.5 13.9 %collective-permute-done = bf16[352,512]{1,0:T(8,128)(2,1)S(1)} collective-permute-done((bf16[352,512]{1,0:T(8,128)(2,1)S(1)}, bf16[352,512]{1,0:T(8,128)(2,1)S(1)}, u32[]{:S(2)}, u32[]{:S(2)}) %collective-permute-start) | collective-permute-done | bytes 360480 | tf_op jit(solution)/shard_map/ppermute | solution.py:22
  51.9 1.6 broadcast_in_dim.7
  53.6 4.0 %all-to-all-start.1 = ((bf16[4,512,512]{2,1,0:T(8,128)(2,1)}), bf16[4,512,512]{2,1,0:T(8,128)(2,1)S(1)}, u32[]{:S(2)}, u32[]{:S(2)}) async-start(bf16[4,512,512]{2,1,0:T(8,128)(2,1)} %broadcast_in_dim.7), calls=%async_computation.1 | async-start | bytes 4194304 | tf_op jit(solution)/shard_map/all_to_all | solution.py:12
  57.6 4.9 %collective-permute-start.3 = (bf16[160,512]{1,0:T(8,128)(2,1)}, bf16[160,512]{1,0:T(8,128)(2,1)S(1)}, u32[]{:S(2)}, u32[]{:S(2)}) collective-permute-start(bf16[160,512]{1,0:T(8,128)(2,1)} %after.4), channel_id=1, source_target_pairs={{0,12},{4,0},{8,4},{12,8},{1,13},{5,1},{9,5},{13,9},{2,14},{6,2},{... | collective-permute-start | bytes 491528 | tf_op jit(solution)/shard_map/ppermute | solution.py:22
  62.5 4.4 %collective-permute-start.2 = (bf16[160,512]{1,0:T(8,128)(2,1)}, bf16[160,512]{1,0:T(8,128)(2,1)S(1)}, u32[]{:S(2)}, u32[]{:S(2)}) collective-permute-start(bf16[160,512]{1,0:T(8,128)(2,1)} %after.3), channel_id=1, source_target_pairs={{0,4},{4,8},{8,12},{12,0},{1,5},{5,9},{9,13},{13,1},{2,6},{6,10},{... | collective-permute-start | bytes 491528 | tf_op jit(solution)/shard_map/ppermute | solution.py:22
  66.9 3.0 %fusion.26 = bf16[256,512]{1,0:T(8,128)(2,1)} fusion(bf16[4,256,512]{2,1,0:T(8,128)(2,1)S(1)} %copy-done.3, bf16[64,4,8,512]{3,2,1,0:T(8,128)(2,1)} %bitcast.115), kind=kOutput, calls=%fused_computation.19 | convolution fusion | flops 537001984 | bytes 3407872 | tf_op jit(solution)/shard_map/dot_general | solution.py:72
  70.0 2.8 %fusion.38 = f32[256,4,512]{2,0,1:T(8,128)} fusion(bf16[4,256,512]{2,1,0:T(8,128)(2,1)S(1)} %copy-done.3, bf16[256,2048]{1,0:T(8,128)(2,1)} %param.3, s32[]{:T(128)S(6)} %dynamic_slice.64), kind=kOutput, calls=%fused_computation.50 | convolution fusion | flops 268435456 | bytes 3276804 | tf_op jit(solution)/shard_map/dot_general | solution.py:84
  72.8 2.8 %fusion.41 = f32[256,4,512]{2,0,1:T(8,128)} fusion(bf16[4,256,512]{2,1,0:T(8,128)(2,1)S(1)} %copy-done.3, bf16[256,2048]{1,0:T(8,128)(2,1)} %param.3, s32[]{:T(128)S(6)} %dynamic_slice.59), kind=kOutput, calls=%fused_computation.53 | convolution fusion | flops 268435456 | bytes 3276804 | tf_op jit(solution)/shard_map/dot_general | solution.py:84
  75.6 1.4 collective-permute-done.2
  77.0 4.6 %collective-permute-start.4 = (bf16[3,64,512]{2,1,0:T(8,128)(2,1)S(1)}, bf16[3,64,512]{2,1,0:T(8,128)(2,1)S(1)}, u32[]{:S(2)}, u32[]{:S(2)}) collective-permute-start(bf16[3,64,512]{2,1,0:T(8,128)(2,1)S(1)} %pad_maximum_fusion.5), channel_id=1, source_target_pairs={{0,3},{1,0},{2,1},{3,2},{4,7},{5,4},{6,5},{7,6},{8,11},{9,8},{10,9... | collective-permute-start | bytes 589832 | tf_op jit(solution)/shard_map/ppermute | solution.py:22
  81.6 2.3 %collective-permute-start.5 = (bf16[3,64,512]{2,1,0:T(8,128)(2,1)S(1)}, bf16[3,64,512]{2,1,0:T(8,128)(2,1)S(1)}, u32[]{:S(2)}, u32[]{:S(2)}) collective-permute-start(bf16[3,64,512]{2,1,0:T(8,128)(2,1)S(1)} %pad_maximum_fusion.5), channel_id=1, source_target_pairs={{0,2},{1,3},{2,0},{3,1},{4,6},{5,7},{6,4},{7,5},{8,10},{9,11},{10,... | collective-permute-start | bytes 589832 | tf_op jit(solution)/shard_map/ppermute | solution.py:22
  83.9 2.6 %collective-permute-start.6 = (bf16[3,64,512]{2,1,0:T(8,128)(2,1)S(1)}, bf16[3,64,512]{2,1,0:T(8,128)(2,1)S(1)}, u32[]{:S(2)}, u32[]{:S(2)}) collective-permute-start(bf16[3,64,512]{2,1,0:T(8,128)(2,1)S(1)} %pad_maximum_fusion.5), channel_id=1, source_target_pairs={{0,1},{1,2},{2,3},{3,0},{4,5},{5,6},{6,7},{7,4},{8,9},{9,10},{10,1... | collective-permute-start | bytes 589832 | tf_op jit(solution)/shard_map/ppermute | solution.py:22
  86.5 0.9 slice.103
  90.7 4.4 %collective-permute-done.6 = bf16[3,64,512]{2,1,0:T(8,128)(2,1)S(1)} collective-permute-done((bf16[3,64,512]{2,1,0:T(8,128)(2,1)S(1)}, bf16[3,64,512]{2,1,0:T(8,128)(2,1)S(1)}, u32[]{:S(2)}, u32[]{:S(2)}) %collective-permute-start.6) | collective-permute-done | bytes 196640 | tf_op jit(solution)/shard_map/ppermute | solution.py:22
  97.3 1.4 copy-done
  98.6 2.1 %broadcast_in_dim.8 = bf16[4,256,512]{2,1,0:T(8,128)(2,1)} broadcast(bf16[256,512]{1,0:T(8,128)(2,1)} %after.5), dimensions={1,2} | broadcast | bytes 1310720 | tf_op jit(solution)/shard_map/broadcast_in_dim | solution.py:17
  100.8 3.5 %all-to-all-start.2 = ((bf16[4,256,512]{2,1,0:T(8,128)(2,1)}), bf16[4,256,512]{2,1,0:T(8,128)(2,1)S(1)}, u32[]{:S(2)}, u32[]{:S(2)}) async-start(bf16[4,256,512]{2,1,0:T(8,128)(2,1)} %broadcast_in_dim.8), calls=%async_computation.2 | async-start | bytes 2097152 | tf_op jit(solution)/shard_map/all_to_all | solution.py:12
  105.7 1.3 dynamic-slice_bitcast_fusion
  108.2 2.1 fusion.14
  110.3 7.1 %all-to-all-done.2 = bf16[4,256,512]{2,1,0:T(8,128)(2,1)S(1)} async-done(((bf16[4,256,512]{2,1,0:T(8,128)(2,1)}), bf16[4,256,512]{2,1,0:T(8,128)(2,1)S(1)}, u32[]{:S(2)}, u32[]{:S(2)}) %all-to-all-start.2) | async-done | bytes 1048608 | tf_op jit(solution)/shard_map/all_to_all | solution.py:12
  117.4 2.4 %fusion.23 = bf16[256,512]{1,0:T(8,128)(2,1)S(1)} fusion(bf16[4,256,512]{2,1,0:T(8,128)(2,1)S(1)} %all-to-all-done.2, bf16[64,4,8,512]{3,2,1,0:T(8,128)(2,1)} %bitcast.116), kind=kOutput, calls=%fused_computation.18 | convolution fusion | flops 537001984 | bytes 3407872 | tf_op jit(solution)/shard_map/dot_general | solution.py:72
  119.9 1.0 copy.68
  120.9 4.3 %all-to-all-start.3 = ((bf16[4,4,64,512]{3,2,1,0:T(8,128)(2,1)}), bf16[4,4,64,512]{3,2,1,0:T(8,128)(2,1)}, u32[]{:S(2)}, u32[]{:S(2)}) async-start(bf16[4,4,64,512]{3,2,1,0:T(8,128)(2,1)} %bitcast.106), calls=%async_computation.3 | async-start | bytes 2097152 | tf_op jit(solution)/shard_map/all_to_all | solution.py:12
  125.2 1.8 fusion.31
  127.1 1.5 fusion.13
  128.6 4.8 %collective-permute-start.7 = (bf16[4,256,512]{2,1,0:T(8,128)(2,1)}, bf16[4,256,512]{2,1,0:T(8,128)(2,1)}, u32[]{:S(2)}, u32[]{:S(2)}) collective-permute-start(bf16[4,256,512]{2,1,0:T(8,128)(2,1)} %fusion.13), channel_id=1, source_target_pairs={{0,64},{64,0},{128,192},{192,128},{256,320},{320,256},{384,448},{4... | collective-permute-start | bytes 3145736 | tf_op jit(solution)/shard_map/ppermute | solution.py:90
  133.4 2.1 %fusion.33 = f32[256,4,512]{2,0,1:T(8,128)} fusion(bf16[4,512,512]{2,1,0:T(8,128)(2,1)S(1)} %copy-done.1, bf16[512,512]{1,0:T(8,128)(2,1)S(1)} %bitcast.111, s32[]{:T(128)S(6)} %select_n.66), kind=kOutput, calls=%fused_computation.33 | convolution fusion | flops 536870912 | bytes 4456452 | tf_op jit(solution)/shard_map/dot_general | solution.py:84
  135.5 1.7 all-to-all-done.3
  137.2 1.4 reduce_sum.12
  138.7 3.1 %fusion.6 = bf16[4,256,512]{2,1,0:T(8,128)(2,1)S(1)} fusion(bf16[4,256,512]{2,1,0:T(8,128)(2,1)} %collective-permute-done.7, bf16[4,256,512]{2,1,0:T(8,128)(2,1)S(1)} %all-to-all-done.2, f32[256,4,512]{2,0,1:T(8,128)} %fusion.41, f32[256,4,512]{2,0,1:T(8,128)} %fusion.33, bf16[256,512]{1,0:T(8,128)(2,1)S(1)} %bitcast.113, s32[]{:T(128)S(6)} %select_n.66), kind=kOutput, calls=%fused_computation.7 | convolution fusion | flops 272105472 | bytes 7471108 | tf_op jit(solution)/shard_map/dot_general | solution.py:84
  141.8 10.1 %collective-permute-start.8 = (bf16[2,1,256,512]{3,2,1,0:T(8,128)(2,1)S(1)}, bf16[2,1,256,512]{3,2,1,0:T(8,128)(2,1)S(1)}, u32[]{:S(2)}, u32[]{:S(2)}) collective-permute-start(bf16[2,1,256,512]{3,2,1,0:T(8,128)(2,1)S(1)} %constant_dynamic-slice_fusion), channel_id=1, source_target_pairs={{0,128},{64,192},{128,0},{192,64},{256,384},{320,448},{384,256},{4... | collective-permute-start | bytes 1572872 | tf_op jit(solution)/shard_map/ppermute | solution.py:90
  152.7 4.2 %all-to-all-start.4 = ((bf16[4,64,512]{2,1,0:T(8,128)(2,1)}), bf16[4,64,512]{2,1,0:T(8,128)(2,1)S(1)}, u32[]{:S(2)}, u32[]{:S(2)}) async-start(bf16[4,64,512]{2,1,0:T(8,128)(2,1)} %constant_dynamic-slice_fusion.1), calls=%async_computation.4 | async-start | bytes 524288 | tf_op jit(solution)/shard_map/all_to_all | solution.py:12
  156.9 13.3 %collective-permute-done.8 = bf16[2,1,256,512]{3,2,1,0:T(8,128)(2,1)S(1)} collective-permute-done((bf16[2,1,256,512]{3,2,1,0:T(8,128)(2,1)S(1)}, bf16[2,1,256,512]{3,2,1,0:T(8,128)(2,1)S(1)}, u32[]{:S(2)}, u32[]{:S(2)}) %collective-permute-start.8) | collective-permute-done | bytes 524320 | tf_op jit(solution)/shard_map/ppermute | solution.py:90
  170.4 1.9 collective-permute-start.9
  172.3 13.5 %collective-permute-done.9 = bf16[1,256,512]{2,1,0:T(8,128)(2,1)S(1)} collective-permute-done((bf16[1,256,512]{2,1,0:T(8,128)(2,1)S(1)}, bf16[1,256,512]{2,1,0:T(8,128)(2,1)S(1)}, u32[]{:S(2)}, u32[]{:S(2)}) %collective-permute-start.9) | collective-permute-done | bytes 262176 | tf_op jit(solution)/shard_map/ppermute | solution.py:90
  185.8 1.9 collective-permute-start.10
  187.8 7.9 %all_to_all.30 = bf16[4,64,512]{2,1,0:T(8,128)(2,1)S(1)} all-to-all(bf16[4,64,512]{2,1,0:T(8,128)(2,1)S(1)} %all-to-all-done.4), channel_id=1, replica_groups=mesh['dp'=8,'gx'=4,'gy'=4,'gz'=4] {'gz'}, dimensions={0} | all-to-all | bytes 524288 | tf_op jit(solution)/shard_map/all_to_all | solution.py:12
  195.7 12.6 %collective-permute-done.10 = bf16[256,512]{1,0:T(8,128)(2,1)S(1)} collective-permute-done((bf16[256,512]{1,0:T(8,128)(2,1)S(1)}, bf16[256,512]{1,0:T(8,128)(2,1)S(1)}, u32[]{:S(2)}, u32[]{:S(2)}) %collective-permute-start.10) | collective-permute-done | bytes 262176 | tf_op jit(solution)/shard_map/ppermute | solution.py:104
  208.3 0.9 convert_element_type.82
  (76 shorter events, 11.4 us)
Async XLA Ops:
  0.6 16.8 %copy-start.5 = (bf16[256,512]{1,0:T(8,128)(2,1)S(1)}, bf16[256,512]{1,0:T(8,128)(2,1)}, u32[]{:S(2)}) copy-start(bf16[256,512]{1,0:T(8,128)(2,1)} %param.4) | copy-start | bytes 786436
  3.8 32.7 %collective-permute-start.1 = (bf16[352,512]{1,0:T(8,128)(2,1)S(1)}, bf16[352,512]{1,0:T(8,128)(2,1)S(1)}, u32[]{:S(2)}, u32[]{:S(2)}) collective-permute-start(bf16[352,512]{1,0:T(8,128)(2,1)S(1)} %pad_maximum_fusion.3), channel_id=1, source_target_pairs={{0,12},{4,0},{8,4},{12,8},{1,13},{5,1},{9,5},{13,9},{2,14},{6,2},{... | collective-permute-start | bytes 1081352 | tf_op jit(solution)/shard_map/ppermute | solution.py:22
  15.5 35.0 %collective-permute-start = (bf16[352,512]{1,0:T(8,128)(2,1)S(1)}, bf16[352,512]{1,0:T(8,128)(2,1)S(1)}, u32[]{:S(2)}, u32[]{:S(2)}) collective-permute-start(bf16[352,512]{1,0:T(8,128)(2,1)S(1)} %pad_maximum_fusion.2), channel_id=1, source_target_pairs={{0,4},{4,8},{8,12},{12,0},{1,5},{5,9},{9,13},{13,1},{2,6},{6,10},{... | collective-permute-start | bytes 1081352 | tf_op jit(solution)/shard_map/ppermute | solution.py:22
  18.5 33.4 %all-to-all-start = ((bf16[4,256,512]{2,1,0:T(8,128)(2,1)}), bf16[4,256,512]{2,1,0:T(8,128)(2,1)S(1)}, u32[]{:S(2)}, u32[]{:S(2)}) async-start(bf16[4,256,512]{2,1,0:T(8,128)(2,1)} %broadcast_in_dim.6), calls=%async_computation | async-start | bytes 2097152 | tf_op jit(solution)/shard_map/all_to_all | solution.py:12
  51.9 1.7 copy-start.2
  53.6 43.7 %all-to-all-start.1 = ((bf16[4,512,512]{2,1,0:T(8,128)(2,1)}), bf16[4,512,512]{2,1,0:T(8,128)(2,1)S(1)}, u32[]{:S(2)}, u32[]{:S(2)}) async-start(bf16[4,512,512]{2,1,0:T(8,128)(2,1)} %broadcast_in_dim.7), calls=%async_computation.1 | async-start | bytes 4194304 | tf_op jit(solution)/shard_map/all_to_all | solution.py:12
  57.6 9.3 %copy-start.3 = (bf16[4,256,512]{2,1,0:T(8,128)(2,1)S(1)}, bf16[4,256,512]{2,1,0:T(8,128)(2,1)}, u32[]{:S(2)}) copy-start(bf16[4,256,512]{2,1,0:T(8,128)(2,1)} %copy-done.2) | copy-start | bytes 3145732
  57.6 18.0 %collective-permute-start.3 = (bf16[160,512]{1,0:T(8,128)(2,1)}, bf16[160,512]{1,0:T(8,128)(2,1)S(1)}, u32[]{:S(2)}, u32[]{:S(2)}) collective-permute-start(bf16[160,512]{1,0:T(8,128)(2,1)} %after.4), channel_id=1, source_target_pairs={{0,12},{4,0},{8,4},{12,8},{1,13},{5,1},{9,5},{13,9},{2,14},{6,2},{... | collective-permute-start | bytes 491528 | tf_op jit(solution)/shard_map/ppermute | solution.py:22
  62.5 14.5 %collective-permute-start.2 = (bf16[160,512]{1,0:T(8,128)(2,1)}, bf16[160,512]{1,0:T(8,128)(2,1)S(1)}, u32[]{:S(2)}, u32[]{:S(2)}) collective-permute-start(bf16[160,512]{1,0:T(8,128)(2,1)} %after.3), channel_id=1, source_target_pairs={{0,4},{4,8},{8,12},{12,0},{1,5},{5,9},{9,13},{13,1},{2,6},{6,10},{... | collective-permute-start | bytes 491528 | tf_op jit(solution)/shard_map/ppermute | solution.py:22
  75.6 1.4 copy-start.11
  77.0 11.9 %collective-permute-start.4 = (bf16[3,64,512]{2,1,0:T(8,128)(2,1)S(1)}, bf16[3,64,512]{2,1,0:T(8,128)(2,1)S(1)}, u32[]{:S(2)}, u32[]{:S(2)}) collective-permute-start(bf16[3,64,512]{2,1,0:T(8,128)(2,1)S(1)} %pad_maximum_fusion.5), channel_id=1, source_target_pairs={{0,3},{1,0},{2,1},{3,2},{4,7},{5,4},{6,5},{7,6},{8,11},{9,8},{10,9... | collective-permute-start | bytes 589832 | tf_op jit(solution)/shard_map/ppermute | solution.py:22
  81.6 8.4 %collective-permute-start.5 = (bf16[3,64,512]{2,1,0:T(8,128)(2,1)S(1)}, bf16[3,64,512]{2,1,0:T(8,128)(2,1)S(1)}, u32[]{:S(2)}, u32[]{:S(2)}) collective-permute-start(bf16[3,64,512]{2,1,0:T(8,128)(2,1)S(1)} %pad_maximum_fusion.5), channel_id=1, source_target_pairs={{0,2},{1,3},{2,0},{3,1},{4,6},{5,7},{6,4},{7,5},{8,10},{9,11},{10,... | collective-permute-start | bytes 589832 | tf_op jit(solution)/shard_map/ppermute | solution.py:22
  83.9 11.2 %collective-permute-start.6 = (bf16[3,64,512]{2,1,0:T(8,128)(2,1)S(1)}, bf16[3,64,512]{2,1,0:T(8,128)(2,1)S(1)}, u32[]{:S(2)}, u32[]{:S(2)}) collective-permute-start(bf16[3,64,512]{2,1,0:T(8,128)(2,1)S(1)} %pad_maximum_fusion.5), channel_id=1, source_target_pairs={{0,1},{1,2},{2,3},{3,0},{4,5},{5,6},{6,7},{7,4},{8,9},{9,10},{10,1... | collective-permute-start | bytes 589832 | tf_op jit(solution)/shard_map/ppermute | solution.py:22
  95.1 1.4 copy-start.7
  97.3 1.4 copy-start
  98.6 6.3 %copy-start.8 = (bf16[3,64,512]{2,1,0:T(8,128)(2,1)S(1)}, bf16[3,64,512]{2,1,0:T(8,128)(2,1)}, u32[]{:S(2)}) copy-start(bf16[3,64,512]{2,1,0:T(8,128)(2,1)} %copy-done.7) | copy-start | bytes 589828
  100.8 16.6 %all-to-all-start.2 = ((bf16[4,256,512]{2,1,0:T(8,128)(2,1)}), bf16[4,256,512]{2,1,0:T(8,128)(2,1)S(1)}, u32[]{:S(2)}, u32[]{:S(2)}) async-start(bf16[4,256,512]{2,1,0:T(8,128)(2,1)} %broadcast_in_dim.8), calls=%async_computation.2 | async-start | bytes 2097152 | tf_op jit(solution)/shard_map/all_to_all | solution.py:12
  105.7 2.3 %copy-start.1 = (bf16[4,512,512]{2,1,0:T(8,128)(2,1)S(1)}, bf16[4,512,512]{2,1,0:T(8,128)(2,1)}, u32[]{:S(2)}) copy-start(bf16[4,512,512]{2,1,0:T(8,128)(2,1)} %copy-done) | copy-start | bytes 6291460
  105.7 2.5 %copy-start.12 = (bf16[512,2048]{1,0:T(8,128)(2,1)S(1)}, bf16[512,2048]{1,0:T(8,128)(2,1)}, u32[]{:S(2)}) copy-start(bf16[512,2048]{1,0:T(8,128)(2,1)} %param.5) | copy-start | bytes 6291460
  117.4 2.4 %copy-start.9 = (bf16[512,512]{1,0:T(8,128)(2,1)S(1)}, bf16[512,512]{1,0:T(8,128)(2,1)}, u32[]{:S(2)}) copy-start(bf16[512,512]{1,0:T(8,128)(2,1)} %fusion.14) | copy-start | bytes 1572868
  117.4 2.4 %copy-start.10 = (bf16[256,512]{1,0:T(8,128)(2,1)S(1)}, bf16[256,512]{1,0:T(8,128)(2,1)}, u32[]{:S(2)}) copy-start(bf16[256,512]{1,0:T(8,128)(2,1)} %fusion.26) | copy-start | bytes 786436
  120.9 16.2 %all-to-all-start.3 = ((bf16[4,4,64,512]{3,2,1,0:T(8,128)(2,1)}), bf16[4,4,64,512]{3,2,1,0:T(8,128)(2,1)}, u32[]{:S(2)}, u32[]{:S(2)}) async-start(bf16[4,4,64,512]{3,2,1,0:T(8,128)(2,1)} %bitcast.106), calls=%async_computation.3 | async-start | bytes 2097152 | tf_op jit(solution)/shard_map/all_to_all | solution.py:12
  125.2 1.8 copy-start.4
  127.1 6.3 %copy-start.6 = (bf16[2,4,64,512]{3,2,1,0:T(8,128)(2,1)S(1)}, bf16[2,4,64,512]{3,2,1,0:T(8,128)(2,1)}, u32[]{:S(2)}) copy-start(bf16[2,4,64,512]{3,2,1,0:T(8,128)(2,1)} %copy.30) | copy-start | bytes 1572868
  128.6 10.1 %collective-permute-start.7 = (bf16[4,256,512]{2,1,0:T(8,128)(2,1)}, bf16[4,256,512]{2,1,0:T(8,128)(2,1)}, u32[]{:S(2)}, u32[]{:S(2)}) collective-permute-start(bf16[4,256,512]{2,1,0:T(8,128)(2,1)} %fusion.13), channel_id=1, source_target_pairs={{0,64},{64,0},{128,192},{192,128},{256,320},{320,256},{384,448},{4... | collective-permute-start | bytes 3145736 | tf_op jit(solution)/shard_map/ppermute | solution.py:90
  141.8 28.3 %collective-permute-start.8 = (bf16[2,1,256,512]{3,2,1,0:T(8,128)(2,1)S(1)}, bf16[2,1,256,512]{3,2,1,0:T(8,128)(2,1)S(1)}, u32[]{:S(2)}, u32[]{:S(2)}) collective-permute-start(bf16[2,1,256,512]{3,2,1,0:T(8,128)(2,1)S(1)} %constant_dynamic-slice_fusion), channel_id=1, source_target_pairs={{0,128},{64,192},{128,0},{192,64},{256,384},{320,448},{384,256},{4... | collective-permute-start | bytes 1572872 | tf_op jit(solution)/shard_map/ppermute | solution.py:90
  152.7 35.1 %all-to-all-start.4 = ((bf16[4,64,512]{2,1,0:T(8,128)(2,1)}), bf16[4,64,512]{2,1,0:T(8,128)(2,1)S(1)}, u32[]{:S(2)}, u32[]{:S(2)}) async-start(bf16[4,64,512]{2,1,0:T(8,128)(2,1)} %constant_dynamic-slice_fusion.1), calls=%async_computation.4 | async-start | bytes 524288 | tf_op jit(solution)/shard_map/all_to_all | solution.py:12
  170.4 15.4 %collective-permute-start.9 = (bf16[1,256,512]{2,1,0:T(8,128)(2,1)S(1)}, bf16[1,256,512]{2,1,0:T(8,128)(2,1)S(1)}, u32[]{:S(2)}, u32[]{:S(2)}) collective-permute-start(bf16[1,256,512]{2,1,0:T(8,128)(2,1)S(1)} %dynamic-slice_bitcast_fusion.1), channel_id=1, source_target_pairs={{0,256},{64,320},{128,384},{192,448},{256,0},{320,64},{384,128},{4... | collective-permute-start | bytes 786440 | tf_op jit(solution)/shard_map/ppermute | solution.py:90
  185.8 22.5 %collective-permute-start.10 = (bf16[256,512]{1,0:T(8,128)(2,1)S(1)}, bf16[256,512]{1,0:T(8,128)(2,1)S(1)}, u32[]{:S(2)}, u32[]{:S(2)}) collective-permute-start(bf16[256,512]{1,0:T(8,128)(2,1)S(1)} %fusion.30), channel_id=1, source_target_pairs={{0,0},{4,128},{8,256},{12,384},{64,64},{68,192},{72,320},{76,448},... | collective-permute-start | bytes 786440 | tf_op jit(solution)/shard_map/ppermute | solution.py:104

commit v3 on v2

--- a/solution.py
+++ b/solution.py
@@ -61,9 +61,11 @@
     via_down = jnp.concatenate([down[:half], down[rows + sub :]], 0)
     far = [shift(after(via_up, b0), "gy", 1), shift(after(via_down, b0), "gy", 3)]
     b13 = gather(jnp.concatenate([up[:rows], down[half:rows], down[:half]], 0), "gx")
-    b2 = gather(after(jnp.concatenate([t[:half] for t in far], 0), b13), "gx")
+    wide = after(jnp.concatenate([t[:half] for t in far], 0), b13[0, :16, :128])
+    wide = jnp.broadcast_to(wide[None], (n, rows, span))
+    b2 = exchange(wide, "gx")
     x = [up[rows : rows + sub], down[rows : rows + sub], jnp.concatenate([t[half:] for t in far], 0)]
-    x = jnp.stack(x)
+    x = after(jnp.stack(x), wide[0, :16, :128])
     x = [x] + [shift(x, "gz", s) for s in (1, 2, 3)]
     x = turned([x[0], x[3], x[2], x[1]], lax.rem(n - gz, n))
     acts = x.transpose(1, 0, 2, 3).reshape(3 * rows, span)
@@ -71,10 +73,6 @@
     terms = [
         lax.dot_general(t, w, (((0, 2), (1, 2)), ((), ())), preferred_element_type=F32).astype(BF16) for t in blocks
     ]
-    terms = jnp.concatenate(terms, 0).reshape(n, n, sub, span).transpose(1, 0, 2, 3)
-    dx = jnp.sum(exchange(terms, "gz").astype(F32), axis=0).astype(BF16)
-    dx = turned([dx[0], dx[2], dx[3], dx[1]], lax.rem(n - me, n))
-    dx = exchange(exchange(dx, "gy"), "gz").reshape(rows, span)
     acts = [block(a, me, span, 1), acts[: 2 * rows], acts[2 * rows :]]
     dp = lax.axis_index("dp")
     core, lo = lax.rem(dp, 2), lax.div(dp, 2)
@@ -84,19 +82,25 @@
             lax.dot_general(block(x, i, rows, 1), t, (((0,), (1,)), ((), ())), preferred_element_type=F32)
             for x, t in zip(acts, blocks)
         )
-        return out.transpose(1, 0, 2).astype(BF16)
+        return out.transpose(1, 0, 2).astype(BF16).reshape(2, 2, rows, span)
 
     def partner(x, bit):
         return lax.ppermute(x, "dp", [(i, i ^ bit) for i in range(8)])
 
-    def added(x, y):
-        return (x.astype(F32) + y.astype(F32)).astype(BF16)
+    def added(*parts):
+        return sum(t.astype(F32) for t in parts).astype(BF16)
 
-    other = partner(share(1 - core), 1)
-    dw = added(share(core), other).reshape(2, 2, rows, span)
+    first = share(1 - core)
+    terms = jnp.concatenate(terms, 0).reshape(n, n, sub, span).transpose(1, 0, 2, 3)
+    dx = jnp.sum(exchange(terms, "gz").astype(F32), axis=0).astype(BF16)
+    dx = turned([dx[0], dx[2], dx[3], dx[1]], lax.rem(n - me, n))
+    dx = exchange(exchange(dx, "gy"), "gz").reshape(rows, span)
+    dw = [share(core), partner(first, 1)]
     low, high = lax.rem(lo, 2), lax.div(lo, 2)
-    dw = added(block(dw, low, 1, 1), partner(block(dw, 1 - low, 1, 1), 2))[:, 0]
-    dw = added(block(dw, high, 1, 0), partner(block(dw, 1 - high, 1, 0), 4))[0]
+    got = partner(added(*(block(t, 1 - low, 1, 1) for t in dw)), 2)
+    dw = [block(t, low, 1, 1) for t in dw] + [got]
+    got = partner(added(*(block(t, 1 - high, 1, 0) for t in dw)), 4)
+    dw = added(*(block(t, high, 1, 0) for t in dw), got)[0, 0]
     swap = [
         ((lo * 2 + c) * 4 + hi, (hi * 2 + c) * 4 + lo)
         for lo in range(4) for c in range(2) for hi in range(4)

time: 211 us -> 200 us (0.948)
  the two profiles are of different devices: /device:TPU:65 before, /device:TPU:98 now
where the time goes in v3:
time: 200 us; the launch traced here: 198 us
  starting transfers between devices  92.5 us (46%)
  waiting for transfers between devices  46.7 us (23%)
  local copies, waits for them, and re-layouts  20.2 us (10%)
  matrix products  18.2 us (9%)
  other arithmetic  10.5 us (5%)
  blocking collectives  9.07 us (5%)
    ppermute x7, starting transfers between devices, shift(): return lax.ppermute(x, axis, [(i, (i + s) % n) for i in range(n)])  37.9 us
    all_to_all x5, starting transfers between devices, exchange(): return lax.all_to_all(x, axis, 0, 0, tiled=True)  29.6 us
    ppermute x7, waiting for transfers between devices, shift(): return lax.ppermute(x, axis, [(i, (i + s) % n) for i in range(n)])  24.7 us
    ppermute x3, starting transfers between devices, partner(): return lax.ppermute(x, 'dp', [(i, i ^ bit) for i in range(8)])  14.4 us
    ppermute x3, waiting for transfers between devices, partner(): return lax.ppermute(x, 'dp', [(i, i ^ bit) for i in range(8)])  10.9 us
    ppermute x1, starting transfers between devices, body(): dw = lax.ppermute(dw, ('dp', 'gy'), swap).astype(F32)  10.6 us
    dot_general x6, matrix products, share(): lax.dot_general(block(x, i, rows, 1), t, (((0,), (1,)), ((), ())), prefer...  10.6 us
    all_to_all x1, blocking collectives, exchange(): return lax.all_to_all(x, axis, 0, 0, tiled=True)  9.07 us
  transfers between devices with their start and end apart: 16, of which 5 were waited for; matrix products, arithmetic and copies ran while one was open for 18% of the time, Pallas kernels for 0%

profile of v3, /device:TPU:98, one launch (start us, length us, event | category | flops | bytes accessed | tf_op | source)
XLA Modules:
  0.0 198.2 jit_solution(9678295208652578252)
XLA Ops:
  0.7 1.0 fusion.51
  1.7 1.1 fusion.50
  2.7 1.0 pad_maximum_fusion.2
  3.7 9.1 %collective-permute-start = (bf16[352,512]{1,0:T(8,128)(2,1)S(1)}, bf16[352,512]{1,0:T(8,128)(2,1)S(1)}, u32[]{:S(2)}, u32[]{:S(2)}) collective-permute-start(bf16[352,512]{1,0:T(8,128)(2,1)S(1)} %pad_maximum_fusion.2), channel_id=1, source_target_pairs={{0,4},{4,8},{8,12},{12,0},{1,5},{5,9},{9,13},{13,1},{2,6},{6,10},{... | collective-permute-start | bytes 1081352 | tf_op jit(solution)/shard_map/ppermute | solution.py:22
  12.8 1.0 fusion.53
  13.8 2.9 %collective-permute-start.1 = (bf16[352,512]{1,0:T(8,128)(2,1)S(1)}, bf16[352,512]{1,0:T(8,128)(2,1)S(1)}, u32[]{:S(2)}, u32[]{:S(2)}) collective-permute-start(bf16[352,512]{1,0:T(8,128)(2,1)S(1)} %pad_maximum_fusion.3), channel_id=1, source_target_pairs={{0,12},{4,0},{8,4},{12,8},{1,13},{5,1},{9,5},{13,9},{2,14},{6,2},{... | collective-permute-start | bytes 1081352 | tf_op jit(solution)/shard_map/ppermute | solution.py:22
  16.7 1.1 broadcast_in_dim.6
  17.8 4.8 %all-to-all-start = ((bf16[4,256,512]{2,1,0:T(8,128)(2,1)}), bf16[4,256,512]{2,1,0:T(8,128)(2,1)S(1)}, u32[]{:S(2)}, u32[]{:S(2)}) async-start(bf16[4,256,512]{2,1,0:T(8,128)(2,1)} %broadcast_in_dim.6), calls=%async_computation | async-start | bytes 2097152 | tf_op jit(solution)/shard_map/all_to_all | solution.py:12
  22.6 22.7 %collective-permute-done = bf16[352,512]{1,0:T(8,128)(2,1)S(1)} collective-permute-done((bf16[352,512]{1,0:T(8,128)(2,1)S(1)}, bf16[352,512]{1,0:T(8,128)(2,1)S(1)}, u32[]{:S(2)}, u32[]{:S(2)}) %collective-permute-start) | collective-permute-done | bytes 360480 | tf_op jit(solution)/shard_map/ppermute | solution.py:22
  47.4 1.6 broadcast_in_dim.7
  49.1 4.8 %all-to-all-start.1 = ((bf16[4,512,512]{2,1,0:T(8,128)(2,1)}), bf16[4,512,512]{2,1,0:T(8,128)(2,1)S(1)}, u32[]{:S(2)}, u32[]{:S(2)}) async-start(bf16[4,512,512]{2,1,0:T(8,128)(2,1)} %broadcast_in_dim.7), calls=%async_computation.1 | async-start | bytes 4194304 | tf_op jit(solution)/shard_map/all_to_all | solution.py:12
  53.9 1.7 pad_maximum_fusion.6.refs_0_
  56.2 7.9 %collective-permute-start.3 = (bf16[160,512]{1,0:T(8,128)(2,1)}, bf16[160,512]{1,0:T(8,128)(2,1)S(1)}, u32[]{:S(2)}, u32[]{:S(2)}) collective-permute-start(bf16[160,512]{1,0:T(8,128)(2,1)} %after.5), channel_id=1, source_target_pairs={{0,12},{4,0},{8,4},{12,8},{1,13},{5,1},{9,5},{13,9},{2,14},{6,2},{... | collective-permute-start | bytes 491528 | tf_op jit(solution)/shard_map/ppermute | solution.py:22
  64.1 7.7 %collective-permute-start.2 = (bf16[160,512]{1,0:T(8,128)(2,1)}, bf16[160,512]{1,0:T(8,128)(2,1)S(1)}, u32[]{:S(2)}, u32[]{:S(2)}) collective-permute-start(bf16[160,512]{1,0:T(8,128)(2,1)} %after.4), channel_id=1, source_target_pairs={{0,4},{4,8},{8,12},{12,0},{1,5},{5,9},{9,13},{13,1},{2,6},{6,10},{... | collective-permute-start | bytes 491528 | tf_op jit(solution)/shard_map/ppermute | solution.py:22
  71.8 2.8 %fusion.35 = f32[256,4,512]{2,0,1:T(8,128)} fusion(bf16[4,256,512]{2,1,0:T(8,128)(2,1)S(1)} %copy-done.1, bf16[256,2048]{1,0:T(8,128)(2,1)} %param.3, s32[]{:T(128)S(6)} %dynamic_slice.81), kind=kOutput, calls=%fused_computation.46 | convolution fusion | flops 268435456 | bytes 3276804 | tf_op jit(solution)/shard_map/dot_general | solution.py:82
  74.6 1.5 fusion.24
  76.2 2.8 %fusion.38 = f32[256,4,512]{2,0,1:T(8,128)} fusion(bf16[4,256,512]{2,1,0:T(8,128)(2,1)S(1)} %copy-done.1, bf16[256,2048]{1,0:T(8,128)(2,1)} %param.3, s32[]{:T(128)S(6)} %dynamic_slice.75), kind=kOutput, calls=%fused_computation.49 | convolution fusion | flops 268435456 | bytes 3276804 | tf_op jit(solution)/shard_map/dot_general | solution.py:82
  79.0 2.0 %collective-permute-done.3 = bf16[160,512]{1,0:T(8,128)(2,1)S(1)} collective-permute-done((bf16[160,512]{1,0:T(8,128)(2,1)}, bf16[160,512]{1,0:T(8,128)(2,1)S(1)}, u32[]{:S(2)}, u32[]{:S(2)}) %collective-permute-start.3) | collective-permute-done | bytes 163872 | tf_op jit(solution)/shard_map/ppermute | solution.py:22
  83.1 1.3 slice.121.refs_1_
  84.4 4.9 %collective-permute-start.4 = (bf16[3,64,512]{2,1,0:T(8,128)(2,1)}, bf16[3,64,512]{2,1,0:T(8,128)(2,1)S(1)}, u32[]{:S(2)}, u32[]{:S(2)}) collective-permute-start(bf16[3,64,512]{2,1,0:T(8,128)(2,1)} %after.7), channel_id=1, source_target_pairs={{0,3},{1,0},{2,1},{3,2},{4,7},{5,4},{6,5},{7,6},{8,11},{9,8},{10,9... | collective-permute-start | bytes 589832 | tf_op jit(solution)/shard_map/ppermute | solution.py:22
  89.3 2.6 %collective-permute-start.5 = (bf16[3,64,512]{2,1,0:T(8,128)(2,1)}, bf16[3,64,512]{2,1,0:T(8,128)(2,1)S(1)}, u32[]{:S(2)}, u32[]{:S(2)}) collective-permute-start(bf16[3,64,512]{2,1,0:T(8,128)(2,1)} %after.7), channel_id=1, source_target_pairs={{0,2},{1,3},{2,0},{3,1},{4,6},{5,7},{6,4},{7,5},{8,10},{9,11},{10,... | collective-permute-start | bytes 589832 | tf_op jit(solution)/shard_map/ppermute | solution.py:22
  91.9 2.9 %collective-permute-start.6 = (bf16[3,64,512]{2,1,0:T(8,128)(2,1)}, bf16[3,64,512]{2,1,0:T(8,128)(2,1)}, u32[]{:S(2)}, u32[]{:S(2)}) collective-permute-start(bf16[3,64,512]{2,1,0:T(8,128)(2,1)} %after.7), channel_id=1, source_target_pairs={{0,1},{1,2},{2,3},{3,0},{4,5},{5,6},{6,7},{7,4},{8,9},{9,10},{10,1... | collective-permute-start | bytes 589832 | tf_op jit(solution)/shard_map/ppermute | solution.py:22
  94.8 2.0 %broadcast_in_dim.8 = bf16[4,256,512]{2,1,0:T(8,128)(2,1)} broadcast(bf16[256,512]{1,0:T(8,128)(2,1)} %after.6), dimensions={1,2} | broadcast | bytes 1310720 | tf_op jit(solution)/shard_map/broadcast_in_dim | solution.py:65
  96.8 4.8 %all-to-all-start.2 = ((bf16[4,256,512]{2,1,0:T(8,128)(2,1)}), bf16[4,256,512]{2,1,0:T(8,128)(2,1)S(1)}, u32[]{:S(2)}, u32[]{:S(2)}) async-start(bf16[4,256,512]{2,1,0:T(8,128)(2,1)} %broadcast_in_dim.8), calls=%async_computation.2 | async-start | bytes 2097152 | tf_op jit(solution)/shard_map/all_to_all | solution.py:12
  101.6 3.7 %fusion.12 = bf16[512,512]{1,0:T(8,128)(2,1)} fusion(bf16[4,512,512]{2,1,0:T(8,128)(2,1)S(1)} %all-to-all-done.1, bf16[64,4,8,512]{3,2,1,0:T(8,128)(2,1)} %bitcast.113), kind=kOutput, calls=%fused_computation.12 | convolution fusion | flops 1074003968 | bytes 4718592 | tf_op jit(solution)/shard_map/dot_general | solution.py:74
  105.4 0.9 bitcast_dynamic-update-slice_fusion
  106.4 0.9 bitcast_dynamic-update-slice_fusion.1
  107.3 1.0 dynamic-slice_bitcast_fusion
  108.3 1.1 slice.122
  110.2 2.1 %fusion.28 = f32[256,4,512]{2,0,1:T(8,128)} fusion(bf16[4,512,512]{2,1,0:T(8,128)(2,1)S(1)} %all-to-all-done.1, bf16[512,512]{1,0:T(8,128)(2,1)S(1)} %bitcast.107, s32[]{:T(128)S(6)} %select_n.87), kind=kOutput, calls=%fused_computation.28 | convolution fusion | flops 536870912 | bytes 4456452 | tf_op jit(solution)/shard_map/dot_general | solution.py:82
  112.4 2.4 %fusion.21 = bf16[256,512]{1,0:T(8,128)(2,1)S(1)} fusion(bf16[4,256,512]{2,1,0:T(8,128)(2,1)S(1)} %all-to-all-done.2, bf16[64,4,8,512]{3,2,1,0:T(8,128)(2,1)} %bitcast.114), kind=kOutput, calls=%fused_computation.15 | convolution fusion | flops 537001984 | bytes 3407872 | tf_op jit(solution)/shard_map/dot_general | solution.py:74
  114.9 1.1 copy.69
  116.0 4.3 %all-to-all-start.3 = ((bf16[4,4,64,512]{3,2,1,0:T(8,128)(2,1)}), bf16[4,4,64,512]{3,2,1,0:T(8,128)(2,1)}, u32[]{:S(2)}, u32[]{:S(2)}) async-start(bf16[4,4,64,512]{3,2,1,0:T(8,128)(2,1)} %bitcast.105), calls=%async_computation.3 | async-start | bytes 2097152 | tf_op jit(solution)/shard_map/all_to_all | solution.py:12
  120.3 1.8 fusion.30
  122.1 1.0 slice.123
  123.6 2.1 %collective-permute-start.7 = (bf16[2,2,256,512]{3,2,1,0:T(8,128)(2,1)S(1)}, bf16[2,2,256,512]{3,2,1,0:T(8,128)(2,1)}, u32[]{:S(2)}, u32[]{:S(2)}) collective-permute-start(bf16[2,2,256,512]{3,2,1,0:T(8,128)(2,1)S(1)} %bitcast.109), channel_id=1, source_target_pairs={{0,64},{64,0},{128,192},{192,128},{256,320},{320,256},{384,448},{4... | collective-permute-start | bytes 3145736 | tf_op jit(solution)/shard_map/ppermute | solution.py:88
  126.2 5.0 %all-to-all-done.3 = bf16[4,4,64,512]{3,2,1,0:T(8,128)(2,1)} async-done(((bf16[4,4,64,512]{3,2,1,0:T(8,128)(2,1)}), bf16[4,4,64,512]{3,2,1,0:T(8,128)(2,1)}, u32[]{:S(2)}, u32[]{:S(2)}) %all-to-all-start.3) | async-done | bytes 1048608 | tf_op jit(solution)/shard_map/all_to_all | solution.py:12
  131.2 1.4 reduce_sum.12
  132.7 1.2 add_convert_fusion.2
  133.9 1.9 collective-permute-start.8
  136.6 10.9 %all-to-all-start.4 = ((bf16[4,64,512]{2,1,0:T(8,128)(2,1)}), bf16[4,64,512]{2,1,0:T(8,128)(2,1)S(1)}, u32[]{:S(2)}, u32[]{:S(2)}) async-start(bf16[4,64,512]{2,1,0:T(8,128)(2,1)} %constant_dynamic-slice_fusion), calls=%async_computation.4 | async-start | bytes 524288 | tf_op jit(solution)/shard_map/all_to_all | solution.py:12
  147.5 1.1 add_convert_fusion.4
  148.6 10.4 %collective-permute-start.9 = (bf16[1,1,256,512]{3,2,1,0:T(8,128)(2,1)S(1)}, bf16[1,1,256,512]{3,2,1,0:T(8,128)(2,1)S(1)}, u32[]{:S(2)}, u32[]{:S(2)}) collective-permute-start(bf16[1,1,256,512]{3,2,1,0:T(8,128)(2,1)S(1)} %add_convert_fusion.4), channel_id=1, source_target_pairs={{0,256},{64,320},{128,384},{192,448},{256,0},{320,64},{384,128},{4... | collective-permute-start | bytes 786440 | tf_op jit(solution)/shard_map/ppermute | solution.py:88
  159.0 10.9 %collective-permute-done.9 = bf16[1,1,256,512]{3,2,1,0:T(8,128)(2,1)S(1)} collective-permute-done((bf16[1,1,256,512]{3,2,1,0:T(8,128)(2,1)S(1)}, bf16[1,1,256,512]{3,2,1,0:T(8,128)(2,1)S(1)}, u32[]{:S(2)}, u32[]{:S(2)}) %collective-permute-start.9) | collective-permute-done | bytes 262176 | tf_op jit(solution)/shard_map/ppermute | solution.py:88
  169.9 1.1 fusion.27
  171.0 10.6 %collective-permute-start.10 = (bf16[256,512]{1,0:T(8,128)(2,1)S(1)}, bf16[256,512]{1,0:T(8,128)(2,1)S(1)}, u32[]{:S(2)}, u32[]{:S(2)}) collective-permute-start(bf16[256,512]{1,0:T(8,128)(2,1)S(1)} %fusion.27), channel_id=1, source_target_pairs={{0,0},{4,128},{8,256},{12,384},{64,64},{68,192},{72,320},{76,448},... | collective-permute-start | bytes 786440 | tf_op jit(solution)/shard_map/ppermute | solution.py:108
  181.6 9.1 %all_to_all.30 = bf16[4,64,512]{2,1,0:T(8,128)(2,1)S(1)} all-to-all(bf16[4,64,512]{2,1,0:T(8,128)(2,1)S(1)} %all-to-all-done.4), channel_id=1, replica_groups=mesh['dp'=8,'gx'=4,'gy'=4,'gz'=4] {'gz'}, dimensions={0} | all-to-all | bytes 524288 | tf_op jit(solution)/shard_map/all_to_all | solution.py:12
  190.6 6.0 %collective-permute-done.10 = bf16[256,512]{1,0:T(8,128)(2,1)S(1)} collective-permute-done((bf16[256,512]{1,0:T(8,128)(2,1)S(1)}, bf16[256,512]{1,0:T(8,128)(2,1)S(1)}, u32[]{:S(2)}, u32[]{:S(2)}) %collective-permute-start.10) | collective-permute-done | bytes 262176 | tf_op jit(solution)/shard_map/ppermute | solution.py:108
  (78 shorter events, 9.2 us)
Async XLA Ops:
  0.6 16.1 %copy-start.6 = (bf16[256,512]{1,0:T(8,128)(2,1)S(1)}, bf16[256,512]{1,0:T(8,128)(2,1)}, u32[]{:S(2)}) copy-start(bf16[256,512]{1,0:T(8,128)(2,1)} %param.4) | copy-start | bytes 786436
  3.7 41.6 %collective-permute-start = (bf16[352,512]{1,0:T(8,128)(2,1)S(1)}, bf16[352,512]{1,0:T(8,128)(2,1)S(1)}, u32[]{:S(2)}, u32[]{:S(2)}) collective-permute-start(bf16[352,512]{1,0:T(8,128)(2,1)S(1)} %pad_maximum_fusion.2), channel_id=1, source_target_pairs={{0,4},{4,8},{8,12},{12,0},{1,5},{5,9},{9,13},{13,1},{2,6},{6,10},{... | collective-permute-start | bytes 1081352 | tf_op jit(solution)/shard_map/ppermute | solution.py:22
  13.8 32.2 %collective-permute-start.1 = (bf16[352,512]{1,0:T(8,128)(2,1)S(1)}, bf16[352,512]{1,0:T(8,128)(2,1)S(1)}, u32[]{:S(2)}, u32[]{:S(2)}) collective-permute-start(bf16[352,512]{1,0:T(8,128)(2,1)S(1)} %pad_maximum_fusion.3), channel_id=1, source_target_pairs={{0,12},{4,0},{8,4},{12,8},{1,13},{5,1},{9,5},{13,9},{2,14},{6,2},{... | collective-permute-start | bytes 1081352 | tf_op jit(solution)/shard_map/ppermute | solution.py:22
  17.8 29.6 %all-to-all-start = ((bf16[4,256,512]{2,1,0:T(8,128)(2,1)}), bf16[4,256,512]{2,1,0:T(8,128)(2,1)S(1)}, u32[]{:S(2)}, u32[]{:S(2)}) async-start(bf16[4,256,512]{2,1,0:T(8,128)(2,1)} %broadcast_in_dim.6), calls=%async_computation | async-start | bytes 2097152 | tf_op jit(solution)/shard_map/all_to_all | solution.py:12
  47.4 1.7 copy-start
  49.1 33.4 %all-to-all-start.1 = ((bf16[4,512,512]{2,1,0:T(8,128)(2,1)}), bf16[4,512,512]{2,1,0:T(8,128)(2,1)S(1)}, u32[]{:S(2)}, u32[]{:S(2)}) async-start(bf16[4,512,512]{2,1,0:T(8,128)(2,1)} %broadcast_in_dim.7), calls=%async_computation.1 | async-start | bytes 4194304 | tf_op jit(solution)/shard_map/all_to_all | solution.py:12
  53.9 17.9 %copy-start.1 = (bf16[4,256,512]{2,1,0:T(8,128)(2,1)S(1)}, bf16[4,256,512]{2,1,0:T(8,128)(2,1)}, u32[]{:S(2)}) copy-start(bf16[4,256,512]{2,1,0:T(8,128)(2,1)} %copy-done) | copy-start | bytes 3145732
  56.2 24.8 %collective-permute-start.3 = (bf16[160,512]{1,0:T(8,128)(2,1)}, bf16[160,512]{1,0:T(8,128)(2,1)S(1)}, u32[]{:S(2)}, u32[]{:S(2)}) collective-permute-start(bf16[160,512]{1,0:T(8,128)(2,1)} %after.5), channel_id=1, source_target_pairs={{0,12},{4,0},{8,4},{12,8},{1,13},{5,1},{9,5},{13,9},{2,14},{6,2},{... | collective-permute-start | bytes 491528 | tf_op jit(solution)/shard_map/ppermute | solution.py:22
  64.1 10.5 %copy-start.12 = (bf16[512,2048]{1,0:T(8,128)(2,1)S(1)}, bf16[512,2048]{1,0:T(8,128)(2,1)}, u32[]{:S(2)}) copy-start(bf16[512,2048]{1,0:T(8,128)(2,1)} %param.5) | copy-start | bytes 6291460
  64.1 16.9 %collective-permute-start.2 = (bf16[160,512]{1,0:T(8,128)(2,1)}, bf16[160,512]{1,0:T(8,128)(2,1)S(1)}, u32[]{:S(2)}, u32[]{:S(2)}) collective-permute-start(bf16[160,512]{1,0:T(8,128)(2,1)} %after.4), channel_id=1, source_target_pairs={{0,4},{4,8},{8,12},{12,0},{1,5},{5,9},{9,13},{13,1},{2,6},{6,10},{... | collective-permute-start | bytes 491528 | tf_op jit(solution)/shard_map/ppermute | solution.py:22
  76.2 4.9 %copy-start.9 = (bf16[1,64,512]{2,1,0:T(8,128)(2,1)S(1)}, bf16[1,64,512]{2,1,0:T(8,128)(2,1)}, u32[]{:S(2)}) copy-start(bf16[1,64,512]{2,1,0:T(8,128)(2,1)} %slice_bitcast_fusion) | copy-start | bytes 196612
  76.2 4.9 %copy-start.10 = (bf16[1,64,512]{2,1,0:T(8,128)(2,1)S(1)}, bf16[1,64,512]{2,1,0:T(8,128)(2,1)}, u32[]{:S(2)}) copy-start(bf16[1,64,512]{2,1,0:T(8,128)(2,1)} %slice_bitcast_fusion.1) | copy-start | bytes 196612
  84.4 20.9 %collective-permute-start.4 = (bf16[3,64,512]{2,1,0:T(8,128)(2,1)}, bf16[3,64,512]{2,1,0:T(8,128)(2,1)S(1)}, u32[]{:S(2)}, u32[]{:S(2)}) collective-permute-start(bf16[3,64,512]{2,1,0:T(8,128)(2,1)} %after.7), channel_id=1, source_target_pairs={{0,3},{1,0},{2,1},{3,2},{4,7},{5,4},{6,5},{7,6},{8,11},{9,8},{10,9... | collective-permute-start | bytes 589832 | tf_op jit(solution)/shard_map/ppermute | solution.py:22
  89.3 16.0 %collective-permute-start.5 = (bf16[3,64,512]{2,1,0:T(8,128)(2,1)}, bf16[3,64,512]{2,1,0:T(8,128)(2,1)S(1)}, u32[]{:S(2)}, u32[]{:S(2)}) collective-permute-start(bf16[3,64,512]{2,1,0:T(8,128)(2,1)} %after.7), channel_id=1, source_target_pairs={{0,2},{1,3},{2,0},{3,1},{4,6},{5,7},{6,4},{7,5},{8,10},{9,11},{10,... | collective-permute-start | bytes 589832 | tf_op jit(solution)/shard_map/ppermute | solution.py:22
  91.9 13.5 %collective-permute-start.6 = (bf16[3,64,512]{2,1,0:T(8,128)(2,1)}, bf16[3,64,512]{2,1,0:T(8,128)(2,1)}, u32[]{:S(2)}, u32[]{:S(2)}) collective-permute-start(bf16[3,64,512]{2,1,0:T(8,128)(2,1)} %after.7), channel_id=1, source_target_pairs={{0,1},{1,2},{2,3},{3,0},{4,5},{5,6},{6,7},{7,4},{8,9},{9,10},{10,1... | collective-permute-start | bytes 589832 | tf_op jit(solution)/shard_map/ppermute | solution.py:22
  96.8 15.6 %all-to-all-start.2 = ((bf16[4,256,512]{2,1,0:T(8,128)(2,1)}), bf16[4,256,512]{2,1,0:T(8,128)(2,1)S(1)}, u32[]{:S(2)}, u32[]{:S(2)}) async-start(bf16[4,256,512]{2,1,0:T(8,128)(2,1)} %broadcast_in_dim.8), calls=%async_computation.2 | async-start | bytes 2097152 | tf_op jit(solution)/shard_map/all_to_all | solution.py:12
  101.6 3.7 %copy-start.5 = (bf16[3,64,512]{2,1,0:T(8,128)(2,1)S(1)}, bf16[3,64,512]{2,1,0:T(8,128)(2,1)}, u32[]{:S(2)}) copy-start(bf16[3,64,512]{2,1,0:T(8,128)(2,1)} %after.7) | copy-start | bytes 589828
  109.4 0.8 copy-start.7
  112.4 2.4 %copy-start.11 = (bf16[256,512]{1,0:T(8,128)(2,1)S(1)}, bf16[256,512]{1,0:T(8,128)(2,1)}, u32[]{:S(2)}) copy-start(bf16[256,512]{1,0:T(8,128)(2,1)} %fusion.24) | copy-start | bytes 786436
  112.4 2.4 %copy-start.8 = (bf16[512,512]{1,0:T(8,128)(2,1)S(1)}, bf16[512,512]{1,0:T(8,128)(2,1)}, u32[]{:S(2)}) copy-start(bf16[512,512]{1,0:T(8,128)(2,1)} %fusion.12) | copy-start | bytes 1572868
  116.0 15.2 %all-to-all-start.3 = ((bf16[4,4,64,512]{3,2,1,0:T(8,128)(2,1)}), bf16[4,4,64,512]{3,2,1,0:T(8,128)(2,1)}, u32[]{:S(2)}, u32[]{:S(2)}) async-start(bf16[4,4,64,512]{3,2,1,0:T(8,128)(2,1)} %bitcast.105), calls=%async_computation.3 | async-start | bytes 2097152 | tf_op jit(solution)/shard_map/all_to_all | solution.py:12
  120.3 2.8 %copy-start.3 = (f32[256,4,512]{2,0,1:T(8,128)S(1)}, f32[256,4,512]{2,0,1:T(8,128)}, u32[]{:S(2)}) copy-start(f32[256,4,512]{2,0,1:T(8,128)} %fusion.35) | copy-start | bytes 6291460
  120.3 2.8 %copy-start.4 = (f32[256,4,512]{2,0,1:T(8,128)S(1)}, f32[256,4,512]{2,0,1:T(8,128)}, u32[]{:S(2)}) copy-start(f32[256,4,512]{2,0,1:T(8,128)} %fusion.28) | copy-start | bytes 6291460
  123.1 2.6 %copy-start.2 = (f32[256,4,512]{2,0,1:T(8,128)S(1)}, f32[256,4,512]{2,0,1:T(8,128)}, u32[]{:S(2)}) copy-start(f32[256,4,512]{2,0,1:T(8,128)} %fusion.38) | copy-start | bytes 6291460
  123.6 9.1 %collective-permute-start.7 = (bf16[2,2,256,512]{3,2,1,0:T(8,128)(2,1)S(1)}, bf16[2,2,256,512]{3,2,1,0:T(8,128)(2,1)}, u32[]{:S(2)}, u32[]{:S(2)}) collective-permute-start(bf16[2,2,256,512]{3,2,1,0:T(8,128)(2,1)S(1)} %bitcast.109), channel_id=1, source_target_pairs={{0,64},{64,0},{128,192},{192,128},{256,320},{320,256},{384,448},{4... | collective-permute-start | bytes 3145736 | tf_op jit(solution)/shard_map/ppermute | solution.py:88
  133.9 13.6 %collective-permute-start.8 = (bf16[2,1,256,512]{3,2,1,0:T(8,128)(2,1)S(1)}, bf16[2,1,256,512]{3,2,1,0:T(8,128)(2,1)S(1)}, u32[]{:S(2)}, u32[]{:S(2)}) collective-permute-start(bf16[2,1,256,512]{3,2,1,0:T(8,128)(2,1)S(1)} %add_convert_fusion.2), channel_id=1, source_target_pairs={{0,128},{64,192},{128,0},{192,64},{256,384},{320,448},{384,256},{4... | collective-permute-start | bytes 1572872 | tf_op jit(solution)/shard_map/ppermute | solution.py:88
  136.6 45.0 %all-to-all-start.4 = ((bf16[4,64,512]{2,1,0:T(8,128)(2,1)}), bf16[4,64,512]{2,1,0:T(8,128)(2,1)S(1)}, u32[]{:S(2)}, u32[]{:S(2)}) async-start(bf16[4,64,512]{2,1,0:T(8,128)(2,1)} %constant_dynamic-slice_fusion), calls=%async_computation.4 | async-start | bytes 524288 | tf_op jit(solution)/shard_map/all_to_all | solution.py:12
  148.6 21.3 %collective-permute-start.9 = (bf16[1,1,256,512]{3,2,1,0:T(8,128)(2,1)S(1)}, bf16[1,1,256,512]{3,2,1,0:T(8,128)(2,1)S(1)}, u32[]{:S(2)}, u32[]{:S(2)}) collective-permute-start(bf16[1,1,256,512]{3,2,1,0:T(8,128)(2,1)S(1)} %add_convert_fusion.4), channel_id=1, source_target_pairs={{0,256},{64,320},{128,384},{192,448},{256,0},{320,64},{384,128},{4... | collective-permute-start | bytes 786440 | tf_op jit(solution)/shard_map/ppermute | solution.py:88
  171.0 25.7 %collective-permute-start.10 = (bf16[256,512]{1,0:T(8,128)(2,1)S(1)}, bf16[256,512]{1,0:T(8,128)(2,1)S(1)}, u32[]{:S(2)}, u32[]{:S(2)}) collective-permute-start(bf16[256,512]{1,0:T(8,128)(2,1)S(1)} %fusion.27), channel_id=1, source_target_pairs={{0,0},{4,128},{8,256},{12,384},{64,64},{68,192},{72,320},{76,448},... | collective-permute-start | bytes 786440 | tf_op jit(solution)/shard_map/ppermute | solution.py:108

commit v4 on v3

--- a/solution.py
+++ b/solution.py
@@ -61,8 +61,8 @@
     via_down = jnp.concatenate([down[:half], down[rows + sub :]], 0)
     far = [shift(after(via_up, b0), "gy", 1), shift(after(via_down, b0), "gy", 3)]
     b13 = gather(jnp.concatenate([up[:rows], down[half:rows], down[:half]], 0), "gx")
-    wide = after(jnp.concatenate([t[:half] for t in far], 0), b13[0, :16, :128])
-    wide = jnp.broadcast_to(wide[None], (n, rows, span))
+    wide = jnp.broadcast_to(jnp.concatenate([t[:half] for t in far], 0)[None], (n, rows, span))
+    wide = after(wide, b13[0, :16, :128])
     b2 = exchange(wide, "gx")
     x = [up[rows : rows + sub], down[rows : rows + sub], jnp.concatenate([t[half:] for t in far], 0)]
     x = after(jnp.stack(x), wide[0, :16, :128])
@@ -91,8 +91,9 @@
         return sum(t.astype(F32) for t in parts).astype(BF16)
 
     first = share(1 - core)
-    terms = jnp.concatenate(terms, 0).reshape(n, n, sub, span).transpose(1, 0, 2, 3)
-    dx = jnp.sum(exchange(terms, "gz").astype(F32), axis=0).astype(BF16)
+    terms = jnp.concatenate(terms, 0).reshape(n, n, sub, span)
+    dx = [block(terms, gz, 1, 1)] + [shift(block(terms, lax.rem(gz + s, n), 1, 1), "gz", s) for s in (1, 2, 3)]
+    dx = sum(t.astype(F32) for t in dx).astype(BF16)[:, 0]
     dx = turned([dx[0], dx[2], dx[3], dx[1]], lax.rem(n - me, n))
     dx = exchange(exchange(dx, "gy"), "gz").reshape(rows, span)
     dw = [share(core), partner(first, 1)]

time: 200 us -> 201 us (level)
  the two profiles are of different devices: /device:TPU:98 before, /device:TPU:65 now
where the time goes in v4:
time: 201 us; the launch traced here: 199 us
  starting transfers between devices  102 us (51%)
  waiting for transfers between devices  49.7 us (25%)
  matrix products  18.6 us (9%)
  local copies, waits for them, and re-layouts  12.6 us (6%)
  blocking collectives  7.92 us (4%)
  other arithmetic  6.35 us (3%)
    ppermute x10, starting transfers between devices, shift(): return lax.ppermute(x, axis, [(i, (i + s) % n) for i in range(n)])  42.8 us
    ppermute x3, starting transfers between devices, partner(): return lax.ppermute(x, 'dp', [(i, i ^ bit) for i in range(8)])  27.5 us
    ppermute x10, waiting for transfers between devices, shift(): return lax.ppermute(x, axis, [(i, (i + s) % n) for i in range(n)])  25.9 us
    all_to_all x4, starting transfers between devices, exchange(): return lax.all_to_all(x, axis, 0, 0, tiled=True)  21.8 us
    ppermute x3, waiting for transfers between devices, partner(): return lax.ppermute(x, 'dp', [(i, i ^ bit) for i in range(8)])  12.6 us
    dot_general x6, matrix products, share(): lax.dot_general(block(x, i, rows, 1), t, (((0,), (1,)), ((), ())), prefer...  10.9 us
    ppermute x1, starting transfers between devices, body(): dw = lax.ppermute(dw, ('dp', 'gy'), swap).astype(F32)  10.1 us
    ppermute x1, waiting for transfers between devices, body(): dw = lax.ppermute(dw, ('dp', 'gy'), swap).astype(F32)  8.06 us
  transfers between devices with their start and end apart: 18, of which 7 were waited for; matrix products, arithmetic and copies ran while one was open for 13% of the time, Pallas kernels for 0%

profile of v4, /device:TPU:65, one launch (start us, length us, event | category | flops | bytes accessed | tf_op | source)
XLA Modules:
  0.0 198.5 jit_solution(4717000920558118080)
XLA Ops:
  0.7 1.0 fusion.59
  1.7 1.1 fusion.58
  2.7 1.0 pad_maximum_fusion.2
  3.7 8.8 %collective-permute-start = (bf16[352,512]{1,0:T(8,128)(2,1)S(1)}, bf16[352,512]{1,0:T(8,128)(2,1)S(1)}, u32[]{:S(2)}, u32[]{:S(2)}) collective-permute-start(bf16[352,512]{1,0:T(8,128)(2,1)S(1)} %pad_maximum_fusion.2), channel_id=1, source_target_pairs={{0,4},{4,8},{8,12},{12,0},{1,5},{5,9},{9,13},{13,1},{2,6},{6,10},{... | collective-permute-start | bytes 1081352 | tf_op jit(solution)/shard_map/ppermute | solution.py:22
  12.5 1.0 fusion.61
  13.6 3.8 %collective-permute-start.1 = (bf16[352,512]{1,0:T(8,128)(2,1)S(1)}, bf16[352,512]{1,0:T(8,128)(2,1)S(1)}, u32[]{:S(2)}, u32[]{:S(2)}) collective-permute-start(bf16[352,512]{1,0:T(8,128)(2,1)S(1)} %pad_maximum_fusion.3), channel_id=1, source_target_pairs={{0,12},{4,0},{8,4},{12,8},{1,13},{5,1},{9,5},{13,9},{2,14},{6,2},{... | collective-permute-start | bytes 1081352 | tf_op jit(solution)/shard_map/ppermute | solution.py:22
  17.4 1.1 broadcast_in_dim.6
  18.4 4.0 %all-to-all-start = ((bf16[4,256,512]{2,1,0:T(8,128)(2,1)}), bf16[4,256,512]{2,1,0:T(8,128)(2,1)S(1)}, u32[]{:S(2)}, u32[]{:S(2)}) async-start(bf16[4,256,512]{2,1,0:T(8,128)(2,1)} %broadcast_in_dim.6), calls=%async_computation | async-start | bytes 2097152 | tf_op jit(solution)/shard_map/all_to_all | solution.py:12
  22.4 19.3 %collective-permute-done = bf16[352,512]{1,0:T(8,128)(2,1)S(1)} collective-permute-done((bf16[352,512]{1,0:T(8,128)(2,1)S(1)}, bf16[352,512]{1,0:T(8,128)(2,1)S(1)}, u32[]{:S(2)}, u32[]{:S(2)}) %collective-permute-start) | collective-permute-done | bytes 360480 | tf_op jit(solution)/shard_map/ppermute | solution.py:22
  42.4 1.4 collective-permute-done.1
  43.8 0.7 pad_maximum_fusion.7.refs_0_
  45.2 1.7 broadcast_in_dim.7
  46.9 4.0 %all-to-all-start.1 = ((bf16[4,512,512]{2,1,0:T(8,128)(2,1)}), bf16[4,512,512]{2,1,0:T(8,128)(2,1)S(1)}, u32[]{:S(2)}, u32[]{:S(2)}) async-start(bf16[4,512,512]{2,1,0:T(8,128)(2,1)} %broadcast_in_dim.7), calls=%async_computation.1 | async-start | bytes 4194304 | tf_op jit(solution)/shard_map/all_to_all | solution.py:12
  50.9 1.7 pad_maximum_fusion.6.refs_0_
  53.2 6.2 %collective-permute-start.3 = (bf16[160,512]{1,0:T(8,128)(2,1)}, bf16[160,512]{1,0:T(8,128)(2,1)S(1)}, u32[]{:S(2)}, u32[]{:S(2)}) collective-permute-start(bf16[160,512]{1,0:T(8,128)(2,1)} %after.5), channel_id=1, source_target_pairs={{0,12},{4,0},{8,4},{12,8},{1,13},{5,1},{9,5},{13,9},{2,14},{6,2},{... | collective-permute-start | bytes 491528 | tf_op jit(solution)/shard_map/ppermute | solution.py:22
  59.4 4.6 %collective-permute-start.2 = (bf16[160,512]{1,0:T(8,128)(2,1)}, bf16[160,512]{1,0:T(8,128)(2,1)S(1)}, u32[]{:S(2)}, u32[]{:S(2)}) collective-permute-start(bf16[160,512]{1,0:T(8,128)(2,1)} %after.4), channel_id=1, source_target_pairs={{0,4},{4,8},{8,12},{12,0},{1,5},{5,9},{9,13},{13,1},{2,6},{6,10},{... | collective-permute-start | bytes 491528 | tf_op jit(solution)/shard_map/ppermute | solution.py:22
  64.0 2.8 %fusion.35 = f32[256,4,512]{2,0,1:T(8,128)} fusion(bf16[4,256,512]{2,1,0:T(8,128)(2,1)S(1)} %copy-done.1, bf16[256,2048]{1,0:T(8,128)(2,1)} %param.3, s32[]{:T(128)S(6)} %dynamic_slice.97), kind=kOutput, calls=%fused_computation.46 | convolution fusion | flops 268435456 | bytes 3276804 | tf_op jit(solution)/shard_map/dot_general | solution.py:82
  66.9 1.5 fusion.24
  68.4 2.8 %fusion.38 = f32[256,4,512]{2,0,1:T(8,128)} fusion(bf16[4,256,512]{2,1,0:T(8,128)(2,1)S(1)} %copy-done.1, bf16[256,2048]{1,0:T(8,128)(2,1)} %param.3, s32[]{:T(128)S(6)} %dynamic_slice.91), kind=kOutput, calls=%fused_computation.49 | convolution fusion | flops 268435456 | bytes 3276804 | tf_op jit(solution)/shard_map/dot_general | solution.py:82
  71.3 0.7 pad_maximum_fusion.5.refs_0_
  72.0 3.1 %all-to-all-done.1 = bf16[4,512,512]{2,1,0:T(8,128)(2,1)S(1)} async-done(((bf16[4,512,512]{2,1,0:T(8,128)(2,1)}), bf16[4,512,512]{2,1,0:T(8,128)(2,1)S(1)}, u32[]{:S(2)}, u32[]{:S(2)}) %all-to-all-start.1) | async-done | bytes 2097184 | tf_op jit(solution)/shard_map/all_to_all | solution.py:12
  75.7 1.1 broadcast_in_dim.8.refs_0_
  76.8 3.5 %all-to-all-start.2 = ((bf16[4,256,512]{2,1,0:T(8,128)(2,1)}), bf16[4,256,512]{2,1,0:T(8,128)(2,1)S(1)}, u32[]{:S(2)}, u32[]{:S(2)}) async-start(bf16[4,256,512]{2,1,0:T(8,128)(2,1)} %after.6), calls=%async_computation.2 | async-start | bytes 2097152 | tf_op jit(solution)/shard_map/all_to_all | solution.py:12
  80.3 1.3 slice_bitcast_fusion.6.refs_1_
  81.6 4.7 %collective-permute-start.7 = (bf16[3,64,512]{2,1,0:T(8,128)(2,1)}, bf16[3,64,512]{2,1,0:T(8,128)(2,1)S(1)}, u32[]{:S(2)}, u32[]{:S(2)}) collective-permute-start(bf16[3,64,512]{2,1,0:T(8,128)(2,1)} %after.7), channel_id=1, source_target_pairs={{0,3},{1,0},{2,1},{3,2},{4,7},{5,4},{6,5},{7,6},{8,11},{9,8},{10,9... | collective-permute-start | bytes 589832 | tf_op jit(solution)/shard_map/ppermute | solution.py:22
  86.3 2.3 %collective-permute-start.8 = (bf16[3,64,512]{2,1,0:T(8,128)(2,1)}, bf16[3,64,512]{2,1,0:T(8,128)(2,1)S(1)}, u32[]{:S(2)}, u32[]{:S(2)}) collective-permute-start(bf16[3,64,512]{2,1,0:T(8,128)(2,1)} %after.7), channel_id=1, source_target_pairs={{0,2},{1,3},{2,0},{3,1},{4,6},{5,7},{6,4},{7,5},{8,10},{9,11},{10,... | collective-permute-start | bytes 589832 | tf_op jit(solution)/shard_map/ppermute | solution.py:22
  88.6 2.6 %collective-permute-start.9 = (bf16[3,64,512]{2,1,0:T(8,128)(2,1)}, bf16[3,64,512]{2,1,0:T(8,128)(2,1)S(1)}, u32[]{:S(2)}, u32[]{:S(2)}) collective-permute-start(bf16[3,64,512]{2,1,0:T(8,128)(2,1)} %after.7), channel_id=1, source_target_pairs={{0,1},{1,2},{2,3},{3,0},{4,5},{5,6},{6,7},{7,4},{8,9},{9,10},{10,1... | collective-permute-start | bytes 589832 | tf_op jit(solution)/shard_map/ppermute | solution.py:22
  91.2 3.7 %fusion.12 = bf16[512,512]{1,0:T(8,128)(2,1)} fusion(bf16[4,512,512]{2,1,0:T(8,128)(2,1)S(1)} %all-to-all-done.1, bf16[64,4,8,512]{3,2,1,0:T(8,128)(2,1)} %bitcast.136), kind=kOutput, calls=%fused_computation.12 | convolution fusion | flops 1074003968 | bytes 4718592 | tf_op jit(solution)/shard_map/dot_general | solution.py:74
  94.9 2.2 %collective-permute-done.9 = bf16[3,64,512]{2,1,0:T(8,128)(2,1)S(1)} collective-permute-done((bf16[3,64,512]{2,1,0:T(8,128)(2,1)}, bf16[3,64,512]{2,1,0:T(8,128)(2,1)S(1)}, u32[]{:S(2)}, u32[]{:S(2)}) %collective-permute-start.9) | collective-permute-done | bytes 196640 | tf_op jit(solution)/shard_map/ppermute | solution.py:22
  97.5 2.1 %fusion.28 = f32[256,4,512]{2,0,1:T(8,128)} fusion(bf16[4,512,512]{2,1,0:T(8,128)(2,1)S(1)} %all-to-all-done.1, bf16[512,512]{1,0:T(8,128)(2,1)S(1)} %bitcast.130, s32[]{:T(128)S(6)} %select_n.103), kind=kOutput, calls=%fused_computation.28 | convolution fusion | flops 536870912 | bytes 4456452 | tf_op jit(solution)/shard_map/dot_general | solution.py:82
  99.6 2.1 %fusion.30 = f32[256,4,512]{2,0,1:T(8,128)} fusion(bf16[4,512,512]{2,1,0:T(8,128)(2,1)S(1)} %all-to-all-done.1, bf16[512,512]{1,0:T(8,128)(2,1)S(1)} %bitcast.131, s32[]{:T(128)S(6)} %select_n.94), kind=kOutput, calls=%fused_computation.30 | convolution fusion | flops 536870912 | bytes 4456452 | tf_op jit(solution)/shard_map/dot_general | solution.py:82
  101.8 2.5 %fusion.21 = bf16[256,512]{1,0:T(8,128)(2,1)S(1)} fusion(bf16[4,256,512]{2,1,0:T(8,128)(2,1)S(1)} %all-to-all-done.2, bf16[64,4,8,512]{3,2,1,0:T(8,128)(2,1)} %bitcast.137), kind=kOutput, calls=%fused_computation.15 | convolution fusion | flops 537001984 | bytes 3407872 | tf_op jit(solution)/shard_map/dot_general | solution.py:74
  104.4 2.3 %collective-permute-start.6 = (bf16[4,1,64,512]{3,2,1,0:T(8,128)(2,1)S(1)}, bf16[4,1,64,512]{3,2,1,0:T(8,128)(2,1)S(1)}, u32[]{:S(2)}, u32[]{:S(2)}) collective-permute-start(bf16[4,1,64,512]{3,2,1,0:T(8,128)(2,1)S(1)} %get-tuple-element.3), channel_id=1, source_target_pairs={{0,3},{1,0},{2,1},{3,2},{4,7},{5,4},{6,5},{7,6},{8,11},{9,8},{10,9... | collective-permute-start | bytes 786440 | tf_op jit(solution)/shard_map/ppermute | solution.py:22
  106.8 4.7 %collective-permute-start.5 = (bf16[4,1,64,512]{3,2,1,0:T(8,128)(2,1)S(1)}, bf16[4,1,64,512]{3,2,1,0:T(8,128)(2,1)S(1)}, u32[]{:S(2)}, u32[]{:S(2)}) collective-permute-start(bf16[4,1,64,512]{3,2,1,0:T(8,128)(2,1)S(1)} %get-tuple-element.4), channel_id=1, source_target_pairs={{0,2},{1,3},{2,0},{3,1},{4,6},{5,7},{6,4},{7,5},{8,10},{9,11},{10,... | collective-permute-start | bytes 786440 | tf_op jit(solution)/shard_map/ppermute | solution.py:22
  111.5 2.8 %collective-permute-start.4 = (bf16[4,1,64,512]{3,2,1,0:T(8,128)(2,1)S(1)}, bf16[4,1,64,512]{3,2,1,0:T(8,128)(2,1)S(1)}, u32[]{:S(2)}, u32[]{:S(2)}) collective-permute-start(bf16[4,1,64,512]{3,2,1,0:T(8,128)(2,1)S(1)} %get-tuple-element.2), channel_id=1, source_target_pairs={{0,1},{1,2},{2,3},{3,0},{4,5},{5,6},{6,7},{7,4},{8,9},{9,10},{10,1... | collective-permute-start | bytes 786440 | tf_op jit(solution)/shard_map/ppermute | solution.py:22
  114.8 5.3 %collective-permute-start.10 = (bf16[2,2,256,512]{3,2,1,0:T(8,128)(2,1)S(1)}, bf16[2,2,256,512]{3,2,1,0:T(8,128)(2,1)S(1)}, u32[]{:S(2)}, u32[]{:S(2)}) collective-permute-start(bf16[2,2,256,512]{3,2,1,0:T(8,128)(2,1)S(1)} %bitcast.132), channel_id=1, source_target_pairs={{0,64},{64,0},{128,192},{192,128},{256,320},{320,256},{384,448},{4... | collective-permute-start | bytes 3145736 | tf_op jit(solution)/shard_map/ppermute | solution.py:88
  120.7 3.0 %collective-permute-done.4 = bf16[4,1,64,512]{3,2,1,0:T(8,128)(2,1)S(1)} collective-permute-done((bf16[4,1,64,512]{3,2,1,0:T(8,128)(2,1)S(1)}, bf16[4,1,64,512]{3,2,1,0:T(8,128)(2,1)S(1)}, u32[]{:S(2)}, u32[]{:S(2)}) %collective-permute-start.4) | collective-permute-done | bytes 262176 | tf_op jit(solution)/shard_map/ppermute | solution.py:22
  123.9 0.9 add_convert_fusion.2
  124.9 7.0 %collective-permute-start.11 = (bf16[2,1,256,512]{3,2,1,0:T(8,128)(2,1)}, bf16[2,1,256,512]{3,2,1,0:T(8,128)(2,1)S(1)}, u32[]{:S(2)}, u32[]{:S(2)}) collective-permute-start(bf16[2,1,256,512]{3,2,1,0:T(8,128)(2,1)} %add_convert_fusion.2), channel_id=1, source_target_pairs={{0,128},{64,192},{128,0},{192,64},{256,384},{320,448},{384,256},{4... | collective-permute-start | bytes 1572872 | tf_op jit(solution)/shard_map/ppermute | solution.py:88
  131.9 0.7 constant_dynamic-slice_fusion
  132.6 10.3 %all-to-all-start.3 = ((bf16[4,64,512]{2,1,0:T(8,128)(2,1)}), bf16[4,64,512]{2,1,0:T(8,128)(2,1)S(1)}, u32[]{:S(2)}, u32[]{:S(2)}) async-start(bf16[4,64,512]{2,1,0:T(8,128)(2,1)} %constant_dynamic-slice_fusion), calls=%async_computation.3 | async-start | bytes 524288 | tf_op jit(solution)/shard_map/all_to_all | solution.py:12
  143.0 15.2 %collective-permute-start.12 = (bf16[1,1,256,512]{3,2,1,0:T(8,128)(2,1)S(1)}, bf16[1,1,256,512]{3,2,1,0:T(8,128)(2,1)S(1)}, u32[]{:S(2)}, u32[]{:S(2)}) collective-permute-start(bf16[1,1,256,512]{3,2,1,0:T(8,128)(2,1)S(1)} %add_convert_fusion.4), channel_id=1, source_target_pairs={{0,256},{64,320},{128,384},{192,448},{256,0},{320,64},{384,128},{4... | collective-permute-start | bytes 786440 | tf_op jit(solution)/shard_map/ppermute | solution.py:88
  158.2 12.6 %collective-permute-done.12 = bf16[1,1,256,512]{3,2,1,0:T(8,128)(2,1)S(1)} collective-permute-done((bf16[1,1,256,512]{3,2,1,0:T(8,128)(2,1)S(1)}, bf16[1,1,256,512]{3,2,1,0:T(8,128)(2,1)S(1)}, u32[]{:S(2)}, u32[]{:S(2)}) %collective-permute-start.12) | collective-permute-done | bytes 262176 | tf_op jit(solution)/shard_map/ppermute | solution.py:88
  170.9 10.1 %collective-permute-start.13 = (bf16[256,512]{1,0:T(8,128)(2,1)S(1)}, bf16[256,512]{1,0:T(8,128)(2,1)S(1)}, u32[]{:S(2)}, u32[]{:S(2)}) collective-permute-start(bf16[256,512]{1,0:T(8,128)(2,1)S(1)} %fusion.27), channel_id=1, source_target_pairs={{0,0},{4,128},{8,256},{12,384},{64,64},{68,192},{72,320},{76,448},... | collective-permute-start | bytes 786440 | tf_op jit(solution)/shard_map/ppermute | solution.py:109
  181.0 7.9 %all_to_all.25 = bf16[4,64,512]{2,1,0:T(8,128)(2,1)S(1)} all-to-all(bf16[4,64,512]{2,1,0:T(8,128)(2,1)S(1)} %all-to-all-done.3), channel_id=1, replica_groups=mesh['dp'=8,'gx'=4,'gy'=4,'gz'=4] {'gz'}, dimensions={0} | all-to-all | bytes 524288 | tf_op jit(solution)/shard_map/all_to_all | solution.py:12
  188.9 8.1 %collective-permute-done.13 = bf16[256,512]{1,0:T(8,128)(2,1)S(1)} collective-permute-done((bf16[256,512]{1,0:T(8,128)(2,1)S(1)}, bf16[256,512]{1,0:T(8,128)(2,1)S(1)}, u32[]{:S(2)}, u32[]{:S(2)}) %collective-permute-start.13) | collective-permute-done | bytes 262176 | tf_op jit(solution)/shard_map/ppermute | solution.py:109
  197.0 0.9 convert_element_type.99
  197.8 0.7 copy.76
  (84 shorter events, 4.6 us)
Async XLA Ops:
  0.6 16.7 %copy-start.7 = (bf16[256,512]{1,0:T(8,128)(2,1)S(1)}, bf16[256,512]{1,0:T(8,128)(2,1)}, u32[]{:S(2)}) copy-start(bf16[256,512]{1,0:T(8,128)(2,1)} %param.4) | copy-start | bytes 786436
  3.7 38.0 %collective-permute-start = (bf16[352,512]{1,0:T(8,128)(2,1)S(1)}, bf16[352,512]{1,0:T(8,128)(2,1)S(1)}, u32[]{:S(2)}, u32[]{:S(2)}) collective-permute-start(bf16[352,512]{1,0:T(8,128)(2,1)S(1)} %pad_maximum_fusion.2), channel_id=1, source_target_pairs={{0,4},{4,8},{8,12},{12,0},{1,5},{5,9},{9,13},{13,1},{2,6},{6,10},{... | collective-permute-start | bytes 1081352 | tf_op jit(solution)/shard_map/ppermute | solution.py:22
  13.6 30.2 %collective-permute-start.1 = (bf16[352,512]{1,0:T(8,128)(2,1)S(1)}, bf16[352,512]{1,0:T(8,128)(2,1)S(1)}, u32[]{:S(2)}, u32[]{:S(2)}) collective-permute-start(bf16[352,512]{1,0:T(8,128)(2,1)S(1)} %pad_maximum_fusion.3), channel_id=1, source_target_pairs={{0,12},{4,0},{8,4},{12,8},{1,13},{5,1},{9,5},{13,9},{2,14},{6,2},{... | collective-permute-start | bytes 1081352 | tf_op jit(solution)/shard_map/ppermute | solution.py:22
  18.4 26.7 %all-to-all-start = ((bf16[4,256,512]{2,1,0:T(8,128)(2,1)}), bf16[4,256,512]{2,1,0:T(8,128)(2,1)S(1)}, u32[]{:S(2)}, u32[]{:S(2)}) async-start(bf16[4,256,512]{2,1,0:T(8,128)(2,1)} %broadcast_in_dim.6), calls=%async_computation | async-start | bytes 2097152 | tf_op jit(solution)/shard_map/all_to_all | solution.py:12
  45.2 1.7 copy-start
  46.9 28.2 %all-to-all-start.1 = ((bf16[4,512,512]{2,1,0:T(8,128)(2,1)}), bf16[4,512,512]{2,1,0:T(8,128)(2,1)S(1)}, u32[]{:S(2)}, u32[]{:S(2)}) async-start(bf16[4,512,512]{2,1,0:T(8,128)(2,1)} %broadcast_in_dim.7), calls=%async_computation.1 | async-start | bytes 4194304 | tf_op jit(solution)/shard_map/all_to_all | solution.py:12
  50.9 13.2 %copy-start.1 = (bf16[4,256,512]{2,1,0:T(8,128)(2,1)S(1)}, bf16[4,256,512]{2,1,0:T(8,128)(2,1)}, u32[]{:S(2)}) copy-start(bf16[4,256,512]{2,1,0:T(8,128)(2,1)} %copy-done) | copy-start | bytes 3145732
  53.2 18.0 %collective-permute-start.3 = (bf16[160,512]{1,0:T(8,128)(2,1)}, bf16[160,512]{1,0:T(8,128)(2,1)S(1)}, u32[]{:S(2)}, u32[]{:S(2)}) collective-permute-start(bf16[160,512]{1,0:T(8,128)(2,1)} %after.5), channel_id=1, source_target_pairs={{0,12},{4,0},{8,4},{12,8},{1,13},{5,1},{9,5},{13,9},{2,14},{6,2},{... | collective-permute-start | bytes 491528 | tf_op jit(solution)/shard_map/ppermute | solution.py:22
  59.4 7.5 %copy-start.12 = (bf16[512,2048]{1,0:T(8,128)(2,1)S(1)}, bf16[512,2048]{1,0:T(8,128)(2,1)}, u32[]{:S(2)}) copy-start(bf16[512,2048]{1,0:T(8,128)(2,1)} %param.5) | copy-start | bytes 6291460
  59.4 11.8 %collective-permute-start.2 = (bf16[160,512]{1,0:T(8,128)(2,1)}, bf16[160,512]{1,0:T(8,128)(2,1)S(1)}, u32[]{:S(2)}, u32[]{:S(2)}) collective-permute-start(bf16[160,512]{1,0:T(8,128)(2,1)} %after.4), channel_id=1, source_target_pairs={{0,4},{4,8},{8,12},{12,0},{1,5},{5,9},{9,13},{13,1},{2,6},{6,10},{... | collective-permute-start | bytes 491528 | tf_op jit(solution)/shard_map/ppermute | solution.py:22
  68.4 2.9 %copy-start.9 = (bf16[1,64,512]{2,1,0:T(8,128)(2,1)S(1)}, bf16[1,64,512]{2,1,0:T(8,128)(2,1)}, u32[]{:S(2)}) copy-start(bf16[1,64,512]{2,1,0:T(8,128)(2,1)} %slice_bitcast_fusion) | copy-start | bytes 196612
  68.4 2.9 %copy-start.10 = (bf16[1,64,512]{2,1,0:T(8,128)(2,1)S(1)}, bf16[1,64,512]{2,1,0:T(8,128)(2,1)}, u32[]{:S(2)}) copy-start(bf16[1,64,512]{2,1,0:T(8,128)(2,1)} %slice_bitcast_fusion.1) | copy-start | bytes 196612
  76.8 25.0 %all-to-all-start.2 = ((bf16[4,256,512]{2,1,0:T(8,128)(2,1)}), bf16[4,256,512]{2,1,0:T(8,128)(2,1)S(1)}, u32[]{:S(2)}, u32[]{:S(2)}) async-start(bf16[4,256,512]{2,1,0:T(8,128)(2,1)} %after.6), calls=%async_computation.2 | async-start | bytes 2097152 | tf_op jit(solution)/shard_map/all_to_all | solution.py:12
  81.5 13.3 %copy-start.6 = (bf16[3,64,512]{2,1,0:T(8,128)(2,1)S(1)}, bf16[3,64,512]{2,1,0:T(8,128)(2,1)}, u32[]{:S(2)}) copy-start(bf16[3,64,512]{2,1,0:T(8,128)(2,1)} %after.7) | copy-start | bytes 589828
  81.6 13.3 %collective-permute-start.7 = (bf16[3,64,512]{2,1,0:T(8,128)(2,1)}, bf16[3,64,512]{2,1,0:T(8,128)(2,1)S(1)}, u32[]{:S(2)}, u32[]{:S(2)}) collective-permute-start(bf16[3,64,512]{2,1,0:T(8,128)(2,1)} %after.7), channel_id=1, source_target_pairs={{0,3},{1,0},{2,1},{3,2},{4,7},{5,4},{6,5},{7,6},{8,11},{9,8},{10,9... | collective-permute-start | bytes 589832 | tf_op jit(solution)/shard_map/ppermute | solution.py:22
  86.3 8.6 %collective-permute-start.8 = (bf16[3,64,512]{2,1,0:T(8,128)(2,1)}, bf16[3,64,512]{2,1,0:T(8,128)(2,1)S(1)}, u32[]{:S(2)}, u32[]{:S(2)}) collective-permute-start(bf16[3,64,512]{2,1,0:T(8,128)(2,1)} %after.7), channel_id=1, source_target_pairs={{0,2},{1,3},{2,0},{3,1},{4,6},{5,7},{6,4},{7,5},{8,10},{9,11},{10,... | collective-permute-start | bytes 589832 | tf_op jit(solution)/shard_map/ppermute | solution.py:22
  88.6 8.6 %collective-permute-start.9 = (bf16[3,64,512]{2,1,0:T(8,128)(2,1)}, bf16[3,64,512]{2,1,0:T(8,128)(2,1)S(1)}, u32[]{:S(2)}, u32[]{:S(2)}) collective-permute-start(bf16[3,64,512]{2,1,0:T(8,128)(2,1)} %after.7), channel_id=1, source_target_pairs={{0,1},{1,2},{2,3},{3,0},{4,5},{5,6},{6,7},{7,4},{8,9},{9,10},{10,1... | collective-permute-start | bytes 589832 | tf_op jit(solution)/shard_map/ppermute | solution.py:22
  101.7 2.5 %copy-start.8 = (bf16[512,512]{1,0:T(8,128)(2,1)S(1)}, bf16[512,512]{1,0:T(8,128)(2,1)}, u32[]{:S(2)}) copy-start(bf16[512,512]{1,0:T(8,128)(2,1)} %fusion.12) | copy-start | bytes 1572868
  101.7 2.5 %copy-start.11 = (bf16[256,512]{1,0:T(8,128)(2,1)S(1)}, bf16[256,512]{1,0:T(8,128)(2,1)}, u32[]{:S(2)}) copy-start(bf16[256,512]{1,0:T(8,128)(2,1)} %fusion.24) | copy-start | bytes 786436
  101.8 12.5 %copy-start.5 = (f32[256,4,512]{2,0,1:T(8,128)S(1)}, f32[256,4,512]{2,0,1:T(8,128)}, u32[]{:S(2)}) copy-start(f32[256,4,512]{2,0,1:T(8,128)} %fusion.28) | copy-start | bytes 6291460
  104.3 10.0 %copy-start.3 = (f32[256,4,512]{2,0,1:T(8,128)S(1)}, f32[256,4,512]{2,0,1:T(8,128)}, u32[]{:S(2)}) copy-start(f32[256,4,512]{2,0,1:T(8,128)} %fusion.35) | copy-start | bytes 6291460
  104.4 16.2 %collective-permute-start.6 = (bf16[4,1,64,512]{3,2,1,0:T(8,128)(2,1)S(1)}, bf16[4,1,64,512]{3,2,1,0:T(8,128)(2,1)S(1)}, u32[]{:S(2)}, u32[]{:S(2)}) collective-permute-start(bf16[4,1,64,512]{3,2,1,0:T(8,128)(2,1)S(1)} %get-tuple-element.3), channel_id=1, source_target_pairs={{0,3},{1,0},{2,1},{3,2},{4,7},{5,4},{6,5},{7,6},{8,11},{9,8},{10,9... | collective-permute-start | bytes 786440 | tf_op jit(solution)/shard_map/ppermute | solution.py:22
  106.8 13.9 %collective-permute-start.5 = (bf16[4,1,64,512]{3,2,1,0:T(8,128)(2,1)S(1)}, bf16[4,1,64,512]{3,2,1,0:T(8,128)(2,1)S(1)}, u32[]{:S(2)}, u32[]{:S(2)}) collective-permute-start(bf16[4,1,64,512]{3,2,1,0:T(8,128)(2,1)S(1)} %get-tuple-element.4), channel_id=1, source_target_pairs={{0,2},{1,3},{2,0},{3,1},{4,6},{5,7},{6,4},{7,5},{8,10},{9,11},{10,... | collective-permute-start | bytes 786440 | tf_op jit(solution)/shard_map/ppermute | solution.py:22
  111.5 12.2 %collective-permute-start.4 = (bf16[4,1,64,512]{3,2,1,0:T(8,128)(2,1)S(1)}, bf16[4,1,64,512]{3,2,1,0:T(8,128)(2,1)S(1)}, u32[]{:S(2)}, u32[]{:S(2)}) collective-permute-start(bf16[4,1,64,512]{3,2,1,0:T(8,128)(2,1)S(1)} %get-tuple-element.2), channel_id=1, source_target_pairs={{0,1},{1,2},{2,3},{3,0},{4,5},{5,6},{6,7},{7,4},{8,9},{9,10},{10,1... | collective-permute-start | bytes 786440 | tf_op jit(solution)/shard_map/ppermute | solution.py:22
  114.3 5.9 %copy-start.2 = (f32[256,4,512]{2,0,1:T(8,128)S(1)}, f32[256,4,512]{2,0,1:T(8,128)}, u32[]{:S(2)}) copy-start(f32[256,4,512]{2,0,1:T(8,128)} %fusion.38) | copy-start | bytes 6291460
  114.3 5.9 %copy-start.4 = (f32[256,4,512]{2,0,1:T(8,128)S(1)}, f32[256,4,512]{2,0,1:T(8,128)}, u32[]{:S(2)}) copy-start(f32[256,4,512]{2,0,1:T(8,128)} %fusion.30) | copy-start | bytes 6291460
  114.8 9.1 %collective-permute-start.10 = (bf16[2,2,256,512]{3,2,1,0:T(8,128)(2,1)S(1)}, bf16[2,2,256,512]{3,2,1,0:T(8,128)(2,1)S(1)}, u32[]{:S(2)}, u32[]{:S(2)}) collective-permute-start(bf16[2,2,256,512]{3,2,1,0:T(8,128)(2,1)S(1)} %bitcast.132), channel_id=1, source_target_pairs={{0,64},{64,0},{128,192},{192,128},{256,320},{320,256},{384,448},{4... | collective-permute-start | bytes 3145736 | tf_op jit(solution)/shard_map/ppermute | solution.py:88
  124.9 18.0 %collective-permute-start.11 = (bf16[2,1,256,512]{3,2,1,0:T(8,128)(2,1)}, bf16[2,1,256,512]{3,2,1,0:T(8,128)(2,1)S(1)}, u32[]{:S(2)}, u32[]{:S(2)}) collective-permute-start(bf16[2,1,256,512]{3,2,1,0:T(8,128)(2,1)} %add_convert_fusion.2), channel_id=1, source_target_pairs={{0,128},{64,192},{128,0},{192,64},{256,384},{320,448},{384,256},{4... | collective-permute-start | bytes 1572872 | tf_op jit(solution)/shard_map/ppermute | solution.py:88
  132.6 48.4 %all-to-all-start.3 = ((bf16[4,64,512]{2,1,0:T(8,128)(2,1)}), bf16[4,64,512]{2,1,0:T(8,128)(2,1)S(1)}, u32[]{:S(2)}, u32[]{:S(2)}) async-start(bf16[4,64,512]{2,1,0:T(8,128)(2,1)} %constant_dynamic-slice_fusion), calls=%async_computation.3 | async-start | bytes 524288 | tf_op jit(solution)/shard_map/all_to_all | solution.py:12
  143.0 27.8 %collective-permute-start.12 = (bf16[1,1,256,512]{3,2,1,0:T(8,128)(2,1)S(1)}, bf16[1,1,256,512]{3,2,1,0:T(8,128)(2,1)S(1)}, u32[]{:S(2)}, u32[]{:S(2)}) collective-permute-start(bf16[1,1,256,512]{3,2,1,0:T(8,128)(2,1)S(1)} %add_convert_fusion.4), channel_id=1, source_target_pairs={{0,256},{64,320},{128,384},{192,448},{256,0},{320,64},{384,128},{4... | collective-permute-start | bytes 786440 | tf_op jit(solution)/shard_map/ppermute | solution.py:88
  170.9 26.1 %collective-permute-start.13 = (bf16[256,512]{1,0:T(8,128)(2,1)S(1)}, bf16[256,512]{1,0:T(8,128)(2,1)S(1)}, u32[]{:S(2)}, u32[]{:S(2)}) collective-permute-start(bf16[256,512]{1,0:T(8,128)(2,1)S(1)} %fusion.27), channel_id=1, source_target_pairs={{0,0},{4,128},{8,256},{12,384},{64,64},{68,192},{72,320},{76,448},... | collective-permute-start | bytes 786440 | tf_op jit(solution)/shard_map/ppermute | solution.py:109

commit v5 on v4

--- a/solution.py
+++ b/solution.py
@@ -55,12 +55,12 @@
 
     far = piece(2)
     up = shift(jnp.concatenate([g, piece(1), far[: sub // 2]], 0), "gy", 1)
-    down = shift(jnp.concatenate([g[half:], g[:half], piece(3), far[sub // 2 :]], 0), "gy", 3)
+    down = shift(jnp.concatenate([g, piece(3), far[sub // 2 :]], 0), "gy", 3)
     b0 = gather(g, "gx")
     via_up = jnp.concatenate([up[:half], up[rows + sub :]], 0)
-    via_down = jnp.concatenate([down[:half], down[rows + sub :]], 0)
+    via_down = jnp.concatenate([down[half:rows], down[rows + sub :]], 0)
     far = [shift(after(via_up, b0), "gy", 1), shift(after(via_down, b0), "gy", 3)]
-    b13 = gather(jnp.concatenate([up[:rows], down[half:rows], down[:half]], 0), "gx")
+    b13 = gather(jnp.concatenate([up[:rows], down[:rows]], 0), "gx")
     wide = jnp.broadcast_to(jnp.concatenate([t[:half] for t in far], 0)[None], (n, rows, span))
     wide = after(wide, b13[0, :16, :128])
     b2 = exchange(wide, "gx")

time: 201 us -> 201 us (level)
  the two profiles are of different devices: /device:TPU:65 before, /device:TPU:99 now
where the time goes in v5:
time: 201 us; the launch traced here: 200 us
  waiting for transfers between devices  86.9 us (43%)
  starting transfers between devices  66.6 us (33%)
  matrix products  18.6 us (9%)
  local copies, waits for them, and re-layouts  12.6 us (6%)
  blocking collectives  7.92 us (4%)
  other arithmetic  6.4 us (3%)
    ppermute x10, waiting for transfers between devices, shift(): return lax.ppermute(x, axis, [(i, (i + s) % n) for i in range(n)])  46 us
    ppermute x10, starting transfers between devices, shift(): return lax.ppermute(x, axis, [(i, (i + s) % n) for i in range(n)])  38.2 us
    ppermute x3, waiting for transfers between devices, partner(): return lax.ppermute(x, 'dp', [(i, i ^ bit) for i in range(8)])  31.1 us
    all_to_all x4, starting transfers between devices, exchange(): return lax.all_to_all(x, axis, 0, 0, tiled=True)  16.2 us
    dot_general x6, matrix products, share(): lax.dot_general(block(x, i, rows, 1), t, (((0,), (1,)), ((), ())), prefer...  10.9 us
    ppermute x1, waiting for transfers between devices, body(): dw = lax.ppermute(dw, ('dp', 'gy'), swap).astype(F32)  9.85 us
    ppermute x3, starting transfers between devices, partner(): return lax.ppermute(x, 'dp', [(i, i ^ bit) for i in range(8)])  8.47 us
    all_to_all x1, blocking collectives, exchange(): return lax.all_to_all(x, axis, 0, 0, tiled=True)  7.92 us
  transfers between devices with their start and end apart: 18, of which 8 were waited for; matrix products, arithmetic and copies ran while one was open for 13% of the time, Pallas kernels for 0%

profile of v5, /device:TPU:99, one launch (start us, length us, event | category | flops | bytes accessed | tf_op | source)
XLA Modules:
  0.0 200.3 jit_solution(9052550625872819211)
XLA Ops:
  0.7 1.0 fusion.61
  1.7 1.1 fusion.60
  2.7 1.0 fusion.27
  3.7 9.8 %collective-permute-start.1 = (bf16[352,512]{1,0:T(8,128)(2,1)S(1)}, bf16[352,512]{1,0:T(8,128)(2,1)S(1)}, u32[]{:S(2)}, u32[]{:S(2)}) collective-permute-start(bf16[352,512]{1,0:T(8,128)(2,1)S(1)} %get-tuple-element.10), channel_id=1, source_target_pairs={{0,12},{4,0},{8,4},{12,8},{1,13},{5,1},{9,5},{13,9},{2,14},{6,2},{... | collective-permute-start | bytes 1081352 | tf_op jit(solution)/shard_map/ppermute | solution.py:22
  13.5 1.9 collective-permute-start
  15.4 2.0 %broadcast_in_dim.6 = bf16[4,256,512]{2,1,0:T(8,128)(2,1)} broadcast(bf16[256,512]{1,0:T(8,128)(2,1)} %param.4), dimensions={1,2} | broadcast | bytes 1310720 | tf_op jit(solution)/shard_map/broadcast_in_dim | solution.py:17
  17.4 4.3 %all-to-all-start = ((bf16[4,256,512]{2,1,0:T(8,128)(2,1)}), bf16[4,256,512]{2,1,0:T(8,128)(2,1)S(1)}, u32[]{:S(2)}, u32[]{:S(2)}) async-start(bf16[4,256,512]{2,1,0:T(8,128)(2,1)} %broadcast_in_dim.6), calls=%async_computation | async-start | bytes 2097152 | tf_op jit(solution)/shard_map/all_to_all | solution.py:12
  21.7 8.1 %collective-permute-done.1 = bf16[352,512]{1,0:T(8,128)(2,1)S(1)} collective-permute-done((bf16[352,512]{1,0:T(8,128)(2,1)S(1)}, bf16[352,512]{1,0:T(8,128)(2,1)S(1)}, u32[]{:S(2)}, u32[]{:S(2)}) %collective-permute-start.1) | collective-permute-done | bytes 360480 | tf_op jit(solution)/shard_map/ppermute | solution.py:22
  29.8 22.5 %collective-permute-done = bf16[352,512]{1,0:T(8,128)(2,1)S(1)} collective-permute-done((bf16[352,512]{1,0:T(8,128)(2,1)S(1)}, bf16[352,512]{1,0:T(8,128)(2,1)S(1)}, u32[]{:S(2)}, u32[]{:S(2)}) %collective-permute-start) | collective-permute-done | bytes 360480 | tf_op jit(solution)/shard_map/ppermute | solution.py:22
  53.0 0.7 pad_maximum_fusion.7.refs_0_
  54.4 1.7 broadcast_in_dim.7
  56.1 4.3 %all-to-all-start.1 = ((bf16[4,512,512]{2,1,0:T(8,128)(2,1)}), bf16[4,512,512]{2,1,0:T(8,128)(2,1)S(1)}, u32[]{:S(2)}, u32[]{:S(2)}) async-start(bf16[4,512,512]{2,1,0:T(8,128)(2,1)} %broadcast_in_dim.7), calls=%async_computation.1 | async-start | bytes 4194304 | tf_op jit(solution)/shard_map/all_to_all | solution.py:12
  60.3 1.7 pad_maximum_fusion.6.refs_0_
  62.6 5.1 %collective-permute-start.3 = (bf16[160,512]{1,0:T(8,128)(2,1)}, bf16[160,512]{1,0:T(8,128)(2,1)S(1)}, u32[]{:S(2)}, u32[]{:S(2)}) collective-permute-start(bf16[160,512]{1,0:T(8,128)(2,1)} %after.5), channel_id=1, source_target_pairs={{0,12},{4,0},{8,4},{12,8},{1,13},{5,1},{9,5},{13,9},{2,14},{6,2},{... | collective-permute-start | bytes 491528 | tf_op jit(solution)/shard_map/ppermute | solution.py:22
  67.8 4.2 %collective-permute-start.2 = (bf16[160,512]{1,0:T(8,128)(2,1)}, bf16[160,512]{1,0:T(8,128)(2,1)S(1)}, u32[]{:S(2)}, u32[]{:S(2)}) collective-permute-start(bf16[160,512]{1,0:T(8,128)(2,1)} %after.4), channel_id=1, source_target_pairs={{0,4},{4,8},{8,12},{12,0},{1,5},{5,9},{9,13},{13,1},{2,6},{6,10},{... | collective-permute-start | bytes 491528 | tf_op jit(solution)/shard_map/ppermute | solution.py:22
  72.0 2.8 %fusion.37 = f32[256,4,512]{2,0,1:T(8,128)} fusion(bf16[4,256,512]{2,1,0:T(8,128)(2,1)S(1)} %copy-done.1, bf16[256,2048]{1,0:T(8,128)(2,1)} %param.3, s32[]{:T(128)S(6)} %dynamic_slice.97), kind=kOutput, calls=%fused_computation.48 | convolution fusion | flops 268435456 | bytes 3276804 | tf_op jit(solution)/shard_map/dot_general | solution.py:82
  74.8 1.5 fusion.24
  76.3 2.8 %fusion.40 = f32[256,4,512]{2,0,1:T(8,128)} fusion(bf16[4,256,512]{2,1,0:T(8,128)(2,1)S(1)} %copy-done.1, bf16[256,2048]{1,0:T(8,128)(2,1)} %param.3, s32[]{:T(128)S(6)} %dynamic_slice.91), kind=kOutput, calls=%fused_computation.51 | convolution fusion | flops 268435456 | bytes 3276804 | tf_op jit(solution)/shard_map/dot_general | solution.py:82
  79.2 5.6 %collective-permute-done.2 = bf16[160,512]{1,0:T(8,128)(2,1)S(1)} collective-permute-done((bf16[160,512]{1,0:T(8,128)(2,1)}, bf16[160,512]{1,0:T(8,128)(2,1)S(1)}, u32[]{:S(2)}, u32[]{:S(2)}) %collective-permute-start.2) | collective-permute-done | bytes 163872 | tf_op jit(solution)/shard_map/ppermute | solution.py:22
  84.8 0.7 pad_maximum_fusion.5.refs_0_
  86.2 1.1 broadcast_in_dim.8.refs_0_
  87.3 4.2 %all-to-all-start.2 = ((bf16[4,256,512]{2,1,0:T(8,128)(2,1)}), bf16[4,256,512]{2,1,0:T(8,128)(2,1)S(1)}, u32[]{:S(2)}, u32[]{:S(2)}) async-start(bf16[4,256,512]{2,1,0:T(8,128)(2,1)} %after.6), calls=%async_computation.2 | async-start | bytes 2097152 | tf_op jit(solution)/shard_map/all_to_all | solution.py:12
  91.5 1.3 slice_bitcast_fusion.6.refs_1_
  92.8 4.7 %collective-permute-start.7 = (bf16[3,64,512]{2,1,0:T(8,128)(2,1)}, bf16[3,64,512]{2,1,0:T(8,128)(2,1)S(1)}, u32[]{:S(2)}, u32[]{:S(2)}) collective-permute-start(bf16[3,64,512]{2,1,0:T(8,128)(2,1)} %after.7), channel_id=1, source_target_pairs={{0,3},{1,0},{2,1},{3,2},{4,7},{5,4},{6,5},{7,6},{8,11},{9,8},{10,9... | collective-permute-start | bytes 589832 | tf_op jit(solution)/shard_map/ppermute | solution.py:22
  97.5 2.3 %collective-permute-start.8 = (bf16[3,64,512]{2,1,0:T(8,128)(2,1)}, bf16[3,64,512]{2,1,0:T(8,128)(2,1)S(1)}, u32[]{:S(2)}, u32[]{:S(2)}) collective-permute-start(bf16[3,64,512]{2,1,0:T(8,128)(2,1)} %after.7), channel_id=1, source_target_pairs={{0,2},{1,3},{2,0},{3,1},{4,6},{5,7},{6,4},{7,5},{8,10},{9,11},{10,... | collective-permute-start | bytes 589832 | tf_op jit(solution)/shard_map/ppermute | solution.py:22
  99.9 2.6 %collective-permute-start.9 = (bf16[3,64,512]{2,1,0:T(8,128)(2,1)}, bf16[3,64,512]{2,1,0:T(8,128)(2,1)S(1)}, u32[]{:S(2)}, u32[]{:S(2)}) collective-permute-start(bf16[3,64,512]{2,1,0:T(8,128)(2,1)} %after.7), channel_id=1, source_target_pairs={{0,1},{1,2},{2,3},{3,0},{4,5},{5,6},{6,7},{7,4},{8,9},{9,10},{10,1... | collective-permute-start | bytes 589832 | tf_op jit(solution)/shard_map/ppermute | solution.py:22
  102.5 3.7 %fusion.12 = bf16[512,512]{1,0:T(8,128)(2,1)} fusion(bf16[4,512,512]{2,1,0:T(8,128)(2,1)S(1)} %all-to-all-done.1, bf16[64,4,8,512]{3,2,1,0:T(8,128)(2,1)} %bitcast.136), kind=kOutput, calls=%fused_computation.12 | convolution fusion | flops 1074003968 | bytes 4718592 | tf_op jit(solution)/shard_map/dot_general | solution.py:74
  106.2 4.6 %collective-permute-done.9 = bf16[3,64,512]{2,1,0:T(8,128)(2,1)S(1)} collective-permute-done((bf16[3,64,512]{2,1,0:T(8,128)(2,1)}, bf16[3,64,512]{2,1,0:T(8,128)(2,1)S(1)}, u32[]{:S(2)}, u32[]{:S(2)}) %collective-permute-start.9) | collective-permute-done | bytes 196640 | tf_op jit(solution)/shard_map/ppermute | solution.py:22
  111.1 2.1 %fusion.30 = f32[256,4,512]{2,0,1:T(8,128)} fusion(bf16[4,512,512]{2,1,0:T(8,128)(2,1)S(1)} %all-to-all-done.1, bf16[512,512]{1,0:T(8,128)(2,1)S(1)} %bitcast.130, s32[]{:T(128)S(6)} %select_n.103), kind=kOutput, calls=%fused_computation.30 | convolution fusion | flops 536870912 | bytes 4456452 | tf_op jit(solution)/shard_map/dot_general | solution.py:82
  113.3 2.1 %fusion.32 = f32[256,4,512]{2,0,1:T(8,128)} fusion(bf16[4,512,512]{2,1,0:T(8,128)(2,1)S(1)} %all-to-all-done.1, bf16[512,512]{1,0:T(8,128)(2,1)S(1)} %bitcast.131, s32[]{:T(128)S(6)} %select_n.94), kind=kOutput, calls=%fused_computation.32 | convolution fusion | flops 536870912 | bytes 4456452 | tf_op jit(solution)/shard_map/dot_general | solution.py:82
  115.4 2.5 %fusion.21 = bf16[256,512]{1,0:T(8,128)(2,1)S(1)} fusion(bf16[4,256,512]{2,1,0:T(8,128)(2,1)S(1)} %all-to-all-done.2, bf16[64,4,8,512]{3,2,1,0:T(8,128)(2,1)} %bitcast.137), kind=kOutput, calls=%fused_computation.15 | convolution fusion | flops 537001984 | bytes 3407872 | tf_op jit(solution)/shard_map/dot_general | solution.py:74
  118.1 2.1 %collective-permute-start.6 = (bf16[4,1,64,512]{3,2,1,0:T(8,128)(2,1)S(1)}, bf16[4,1,64,512]{3,2,1,0:T(8,128)(2,1)S(1)}, u32[]{:S(2)}, u32[]{:S(2)}) collective-permute-start(bf16[4,1,64,512]{3,2,1,0:T(8,128)(2,1)S(1)} %get-tuple-element.3), channel_id=1, source_target_pairs={{0,3},{1,0},{2,1},{3,2},{4,7},{5,4},{6,5},{7,6},{8,11},{9,8},{10,9... | collective-permute-start | bytes 786440 | tf_op jit(solution)/shard_map/ppermute | solution.py:22
  120.1 2.8 %collective-permute-start.5 = (bf16[4,1,64,512]{3,2,1,0:T(8,128)(2,1)S(1)}, bf16[4,1,64,512]{3,2,1,0:T(8,128)(2,1)S(1)}, u32[]{:S(2)}, u32[]{:S(2)}) collective-permute-start(bf16[4,1,64,512]{3,2,1,0:T(8,128)(2,1)S(1)} %get-tuple-element.4), channel_id=1, source_target_pairs={{0,2},{1,3},{2,0},{3,1},{4,6},{5,7},{6,4},{7,5},{8,10},{9,11},{10,... | collective-permute-start | bytes 786440 | tf_op jit(solution)/shard_map/ppermute | solution.py:22
  122.9 2.8 %collective-permute-start.4 = (bf16[4,1,64,512]{3,2,1,0:T(8,128)(2,1)S(1)}, bf16[4,1,64,512]{3,2,1,0:T(8,128)(2,1)S(1)}, u32[]{:S(2)}, u32[]{:S(2)}) collective-permute-start(bf16[4,1,64,512]{3,2,1,0:T(8,128)(2,1)S(1)} %get-tuple-element.2), channel_id=1, source_target_pairs={{0,1},{1,2},{2,3},{3,0},{4,5},{5,6},{6,7},{7,4},{8,9},{9,10},{10,1... | collective-permute-start | bytes 786440 | tf_op jit(solution)/shard_map/ppermute | solution.py:22
  126.2 4.6 %collective-permute-start.10 = (bf16[2,2,256,512]{3,2,1,0:T(8,128)(2,1)S(1)}, bf16[2,2,256,512]{3,2,1,0:T(8,128)(2,1)S(1)}, u32[]{:S(2)}, u32[]{:S(2)}) collective-permute-start(bf16[2,2,256,512]{3,2,1,0:T(8,128)(2,1)S(1)} %bitcast.132), channel_id=1, source_target_pairs={{0,64},{64,0},{128,192},{192,128},{256,320},{320,256},{384,448},{4... | collective-permute-start | bytes 3145736 | tf_op jit(solution)/shard_map/ppermute | solution.py:88
  131.4 5.2 %collective-permute-done.4 = bf16[4,1,64,512]{3,2,1,0:T(8,128)(2,1)S(1)} collective-permute-done((bf16[4,1,64,512]{3,2,1,0:T(8,128)(2,1)S(1)}, bf16[4,1,64,512]{3,2,1,0:T(8,128)(2,1)S(1)}, u32[]{:S(2)}, u32[]{:S(2)}) %collective-permute-start.4) | collective-permute-done | bytes 262176 | tf_op jit(solution)/shard_map/ppermute | solution.py:22
  136.9 0.9 add_convert_fusion.2
  137.8 1.9 collective-permute-start.11
  139.7 0.7 constant_dynamic-slice_fusion
  140.5 3.4 %all-to-all-start.3 = ((bf16[4,64,512]{2,1,0:T(8,128)(2,1)}), bf16[4,64,512]{2,1,0:T(8,128)(2,1)S(1)}, u32[]{:S(2)}, u32[]{:S(2)}) async-start(bf16[4,64,512]{2,1,0:T(8,128)(2,1)} %constant_dynamic-slice_fusion), calls=%async_computation.3 | async-start | bytes 524288 | tf_op jit(solution)/shard_map/all_to_all | solution.py:12
  143.9 14.5 %collective-permute-done.11 = bf16[2,1,256,512]{3,2,1,0:T(8,128)(2,1)S(1)} collective-permute-done((bf16[2,1,256,512]{3,2,1,0:T(8,128)(2,1)}, bf16[2,1,256,512]{3,2,1,0:T(8,128)(2,1)S(1)}, u32[]{:S(2)}, u32[]{:S(2)}) %collective-permute-start.11) | collective-permute-done | bytes 524320 | tf_op jit(solution)/shard_map/ppermute | solution.py:88
  158.6 1.9 collective-permute-start.12
  160.5 16.6 %collective-permute-done.12 = bf16[1,1,256,512]{3,2,1,0:T(8,128)(2,1)S(1)} collective-permute-done((bf16[1,1,256,512]{3,2,1,0:T(8,128)(2,1)S(1)}, bf16[1,1,256,512]{3,2,1,0:T(8,128)(2,1)S(1)}, u32[]{:S(2)}, u32[]{:S(2)}) %collective-permute-start.12) | collective-permute-done | bytes 262176 | tf_op jit(solution)/shard_map/ppermute | solution.py:88
  177.2 3.7 %collective-permute-start.13 = (bf16[256,512]{1,0:T(8,128)(2,1)S(1)}, bf16[256,512]{1,0:T(8,128)(2,1)S(1)}, u32[]{:S(2)}, u32[]{:S(2)}) collective-permute-start(bf16[256,512]{1,0:T(8,128)(2,1)S(1)} %fusion.29), channel_id=1, source_target_pairs={{0,0},{4,128},{8,256},{12,384},{64,64},{68,192},{72,320},{76,448},... | collective-permute-start | bytes 786440 | tf_op jit(solution)/shard_map/ppermute | solution.py:109
  180.9 7.9 %all_to_all.25 = bf16[4,64,512]{2,1,0:T(8,128)(2,1)S(1)} all-to-all(bf16[4,64,512]{2,1,0:T(8,128)(2,1)S(1)} %all-to-all-done.3), channel_id=1, replica_groups=mesh['dp'=8,'gx'=4,'gy'=4,'gz'=4] {'gz'}, dimensions={0} | all-to-all | bytes 524288 | tf_op jit(solution)/shard_map/all_to_all | solution.py:12
  188.8 9.9 %collective-permute-done.13 = bf16[256,512]{1,0:T(8,128)(2,1)S(1)} collective-permute-done((bf16[256,512]{1,0:T(8,128)(2,1)S(1)}, bf16[256,512]{1,0:T(8,128)(2,1)S(1)}, u32[]{:S(2)}, u32[]{:S(2)}) %collective-permute-start.13) | collective-permute-done | bytes 262176 | tf_op jit(solution)/shard_map/ppermute | solution.py:109
  198.7 0.9 convert_element_type.99
  199.6 0.7 copy.76
  (81 shorter events, 4.6 us)
Async XLA Ops:
  3.7 26.0 %collective-permute-start.1 = (bf16[352,512]{1,0:T(8,128)(2,1)S(1)}, bf16[352,512]{1,0:T(8,128)(2,1)S(1)}, u32[]{:S(2)}, u32[]{:S(2)}) collective-permute-start(bf16[352,512]{1,0:T(8,128)(2,1)S(1)} %get-tuple-element.10), channel_id=1, source_target_pairs={{0,12},{4,0},{8,4},{12,8},{1,13},{5,1},{9,5},{13,9},{2,14},{6,2},{... | collective-permute-start | bytes 1081352 | tf_op jit(solution)/shard_map/ppermute | solution.py:22
  13.5 38.8 %collective-permute-start = (bf16[352,512]{1,0:T(8,128)(2,1)S(1)}, bf16[352,512]{1,0:T(8,128)(2,1)S(1)}, u32[]{:S(2)}, u32[]{:S(2)}) collective-permute-start(bf16[352,512]{1,0:T(8,128)(2,1)S(1)} %get-tuple-element.9), channel_id=1, source_target_pairs={{0,4},{4,8},{8,12},{12,0},{1,5},{5,9},{9,13},{13,1},{2,6},{6,10},{... | collective-permute-start | bytes 1081352 | tf_op jit(solution)/shard_map/ppermute | solution.py:22
  17.4 36.9 %all-to-all-start = ((bf16[4,256,512]{2,1,0:T(8,128)(2,1)}), bf16[4,256,512]{2,1,0:T(8,128)(2,1)S(1)}, u32[]{:S(2)}, u32[]{:S(2)}) async-start(bf16[4,256,512]{2,1,0:T(8,128)(2,1)} %broadcast_in_dim.6), calls=%async_computation | async-start | bytes 2097152 | tf_op jit(solution)/shard_map/all_to_all | solution.py:12
  54.4 1.7 copy-start
  56.1 29.5 %all-to-all-start.1 = ((bf16[4,512,512]{2,1,0:T(8,128)(2,1)}), bf16[4,512,512]{2,1,0:T(8,128)(2,1)S(1)}, u32[]{:S(2)}, u32[]{:S(2)}) async-start(bf16[4,512,512]{2,1,0:T(8,128)(2,1)} %broadcast_in_dim.7), calls=%async_computation.1 | async-start | bytes 4194304 | tf_op jit(solution)/shard_map/all_to_all | solution.py:12
  60.3 11.7 %copy-start.1 = (bf16[4,256,512]{2,1,0:T(8,128)(2,1)S(1)}, bf16[4,256,512]{2,1,0:T(8,128)(2,1)}, u32[]{:S(2)}) copy-start(bf16[4,256,512]{2,1,0:T(8,128)(2,1)} %copy-done) | copy-start | bytes 3145732
  62.6 16.5 %collective-permute-start.3 = (bf16[160,512]{1,0:T(8,128)(2,1)}, bf16[160,512]{1,0:T(8,128)(2,1)S(1)}, u32[]{:S(2)}, u32[]{:S(2)}) collective-permute-start(bf16[160,512]{1,0:T(8,128)(2,1)} %after.5), channel_id=1, source_target_pairs={{0,12},{4,0},{8,4},{12,8},{1,13},{5,1},{9,5},{13,9},{2,14},{6,2},{... | collective-permute-start | bytes 491528 | tf_op jit(solution)/shard_map/ppermute | solution.py:22
  67.8 7.0 %copy-start.11 = (bf16[512,2048]{1,0:T(8,128)(2,1)S(1)}, bf16[512,2048]{1,0:T(8,128)(2,1)}, u32[]{:S(2)}) copy-start(bf16[512,2048]{1,0:T(8,128)(2,1)} %param.5) | copy-start | bytes 6291460
  67.8 16.9 %collective-permute-start.2 = (bf16[160,512]{1,0:T(8,128)(2,1)}, bf16[160,512]{1,0:T(8,128)(2,1)S(1)}, u32[]{:S(2)}, u32[]{:S(2)}) collective-permute-start(bf16[160,512]{1,0:T(8,128)(2,1)} %after.4), channel_id=1, source_target_pairs={{0,4},{4,8},{8,12},{12,0},{1,5},{5,9},{9,13},{13,1},{2,6},{6,10},{... | collective-permute-start | bytes 491528 | tf_op jit(solution)/shard_map/ppermute | solution.py:22
  76.3 8.5 %copy-start.8 = (bf16[1,64,512]{2,1,0:T(8,128)(2,1)S(1)}, bf16[1,64,512]{2,1,0:T(8,128)(2,1)}, u32[]{:S(2)}) copy-start(bf16[1,64,512]{2,1,0:T(8,128)(2,1)} %slice_bitcast_fusion) | copy-start | bytes 196612
  76.3 8.5 %copy-start.9 = (bf16[1,64,512]{2,1,0:T(8,128)(2,1)S(1)}, bf16[1,64,512]{2,1,0:T(8,128)(2,1)}, u32[]{:S(2)}) copy-start(bf16[1,64,512]{2,1,0:T(8,128)(2,1)} %slice_bitcast_fusion.1) | copy-start | bytes 196612
  87.3 28.1 %all-to-all-start.2 = ((bf16[4,256,512]{2,1,0:T(8,128)(2,1)}), bf16[4,256,512]{2,1,0:T(8,128)(2,1)S(1)}, u32[]{:S(2)}, u32[]{:S(2)}) async-start(bf16[4,256,512]{2,1,0:T(8,128)(2,1)} %after.6), calls=%async_computation.2 | async-start | bytes 2097152 | tf_op jit(solution)/shard_map/all_to_all | solution.py:12
  92.8 13.3 %copy-start.6 = (bf16[3,64,512]{2,1,0:T(8,128)(2,1)S(1)}, bf16[3,64,512]{2,1,0:T(8,128)(2,1)}, u32[]{:S(2)}) copy-start(bf16[3,64,512]{2,1,0:T(8,128)(2,1)} %after.7) | copy-start | bytes 589828
  92.8 13.3 %collective-permute-start.7 = (bf16[3,64,512]{2,1,0:T(8,128)(2,1)}, bf16[3,64,512]{2,1,0:T(8,128)(2,1)S(1)}, u32[]{:S(2)}, u32[]{:S(2)}) collective-permute-start(bf16[3,64,512]{2,1,0:T(8,128)(2,1)} %after.7), channel_id=1, source_target_pairs={{0,3},{1,0},{2,1},{3,2},{4,7},{5,4},{6,5},{7,6},{8,11},{9,8},{10,9... | collective-permute-start | bytes 589832 | tf_op jit(solution)/shard_map/ppermute | solution.py:22
  97.5 8.7 %collective-permute-start.8 = (bf16[3,64,512]{2,1,0:T(8,128)(2,1)}, bf16[3,64,512]{2,1,0:T(8,128)(2,1)S(1)}, u32[]{:S(2)}, u32[]{:S(2)}) collective-permute-start(bf16[3,64,512]{2,1,0:T(8,128)(2,1)} %after.7), channel_id=1, source_target_pairs={{0,2},{1,3},{2,0},{3,1},{4,6},{5,7},{6,4},{7,5},{8,10},{9,11},{10,... | collective-permute-start | bytes 589832 | tf_op jit(solution)/shard_map/ppermute | solution.py:22
  99.9 11.0 %collective-permute-start.9 = (bf16[3,64,512]{2,1,0:T(8,128)(2,1)}, bf16[3,64,512]{2,1,0:T(8,128)(2,1)S(1)}, u32[]{:S(2)}, u32[]{:S(2)}) collective-permute-start(bf16[3,64,512]{2,1,0:T(8,128)(2,1)} %after.7), channel_id=1, source_target_pairs={{0,1},{1,2},{2,3},{3,0},{4,5},{5,6},{6,7},{7,4},{8,9},{9,10},{10,1... | collective-permute-start | bytes 589832 | tf_op jit(solution)/shard_map/ppermute | solution.py:22
  115.4 2.5 %copy-start.7 = (bf16[512,512]{1,0:T(8,128)(2,1)S(1)}, bf16[512,512]{1,0:T(8,128)(2,1)}, u32[]{:S(2)}) copy-start(bf16[512,512]{1,0:T(8,128)(2,1)} %fusion.12) | copy-start | bytes 1572868
  115.4 2.5 %copy-start.10 = (bf16[256,512]{1,0:T(8,128)(2,1)S(1)}, bf16[256,512]{1,0:T(8,128)(2,1)}, u32[]{:S(2)}) copy-start(bf16[256,512]{1,0:T(8,128)(2,1)} %fusion.24) | copy-start | bytes 786436
  115.4 10.3 %copy-start.5 = (f32[256,4,512]{2,0,1:T(8,128)S(1)}, f32[256,4,512]{2,0,1:T(8,128)}, u32[]{:S(2)}) copy-start(f32[256,4,512]{2,0,1:T(8,128)} %fusion.30) | copy-start | bytes 6291460
  117.9 7.8 %copy-start.3 = (f32[256,4,512]{2,0,1:T(8,128)S(1)}, f32[256,4,512]{2,0,1:T(8,128)}, u32[]{:S(2)}) copy-start(f32[256,4,512]{2,0,1:T(8,128)} %fusion.37) | copy-start | bytes 6291460
  118.1 13.3 %collective-permute-start.6 = (bf16[4,1,64,512]{3,2,1,0:T(8,128)(2,1)S(1)}, bf16[4,1,64,512]{3,2,1,0:T(8,128)(2,1)S(1)}, u32[]{:S(2)}, u32[]{:S(2)}) collective-permute-start(bf16[4,1,64,512]{3,2,1,0:T(8,128)(2,1)S(1)} %get-tuple-element.3), channel_id=1, source_target_pairs={{0,3},{1,0},{2,1},{3,2},{4,7},{5,4},{6,5},{7,6},{8,11},{9,8},{10,9... | collective-permute-start | bytes 786440 | tf_op jit(solution)/shard_map/ppermute | solution.py:22
  120.1 11.3 %collective-permute-start.5 = (bf16[4,1,64,512]{3,2,1,0:T(8,128)(2,1)S(1)}, bf16[4,1,64,512]{3,2,1,0:T(8,128)(2,1)S(1)}, u32[]{:S(2)}, u32[]{:S(2)}) collective-permute-start(bf16[4,1,64,512]{3,2,1,0:T(8,128)(2,1)S(1)} %get-tuple-element.4), channel_id=1, source_target_pairs={{0,2},{1,3},{2,0},{3,1},{4,6},{5,7},{6,4},{7,5},{8,10},{9,11},{10,... | collective-permute-start | bytes 786440 | tf_op jit(solution)/shard_map/ppermute | solution.py:22
  122.9 13.7 %collective-permute-start.4 = (bf16[4,1,64,512]{3,2,1,0:T(8,128)(2,1)S(1)}, bf16[4,1,64,512]{3,2,1,0:T(8,128)(2,1)S(1)}, u32[]{:S(2)}, u32[]{:S(2)}) collective-permute-start(bf16[4,1,64,512]{3,2,1,0:T(8,128)(2,1)S(1)} %get-tuple-element.2), channel_id=1, source_target_pairs={{0,1},{1,2},{2,3},{3,0},{4,5},{5,6},{6,7},{7,4},{8,9},{9,10},{10,1... | collective-permute-start | bytes 786440 | tf_op jit(solution)/shard_map/ppermute | solution.py:22
  125.7 5.2 %copy-start.2 = (f32[256,4,512]{2,0,1:T(8,128)S(1)}, f32[256,4,512]{2,0,1:T(8,128)}, u32[]{:S(2)}) copy-start(f32[256,4,512]{2,0,1:T(8,128)} %fusion.40) | copy-start | bytes 6291460
  125.7 5.2 %copy-start.4 = (f32[256,4,512]{2,0,1:T(8,128)S(1)}, f32[256,4,512]{2,0,1:T(8,128)}, u32[]{:S(2)}) copy-start(f32[256,4,512]{2,0,1:T(8,128)} %fusion.32) | copy-start | bytes 6291460
  126.2 10.6 %collective-permute-start.10 = (bf16[2,2,256,512]{3,2,1,0:T(8,128)(2,1)S(1)}, bf16[2,2,256,512]{3,2,1,0:T(8,128)(2,1)S(1)}, u32[]{:S(2)}, u32[]{:S(2)}) collective-permute-start(bf16[2,2,256,512]{3,2,1,0:T(8,128)(2,1)S(1)} %bitcast.132), channel_id=1, source_target_pairs={{0,64},{64,0},{128,192},{192,128},{256,320},{320,256},{384,448},{4... | collective-permute-start | bytes 3145736 | tf_op jit(solution)/shard_map/ppermute | solution.py:88
  137.8 20.6 %collective-permute-start.11 = (bf16[2,1,256,512]{3,2,1,0:T(8,128)(2,1)}, bf16[2,1,256,512]{3,2,1,0:T(8,128)(2,1)S(1)}, u32[]{:S(2)}, u32[]{:S(2)}) collective-permute-start(bf16[2,1,256,512]{3,2,1,0:T(8,128)(2,1)} %add_convert_fusion.2), channel_id=1, source_target_pairs={{0,128},{64,192},{128,0},{192,64},{256,384},{320,448},{384,256},{4... | collective-permute-start | bytes 1572872 | tf_op jit(solution)/shard_map/ppermute | solution.py:88
  140.5 40.4 %all-to-all-start.3 = ((bf16[4,64,512]{2,1,0:T(8,128)(2,1)}), bf16[4,64,512]{2,1,0:T(8,128)(2,1)S(1)}, u32[]{:S(2)}, u32[]{:S(2)}) async-start(bf16[4,64,512]{2,1,0:T(8,128)(2,1)} %constant_dynamic-slice_fusion), calls=%async_computation.3 | async-start | bytes 524288 | tf_op jit(solution)/shard_map/all_to_all | solution.py:12
  158.6 18.5 %collective-permute-start.12 = (bf16[1,1,256,512]{3,2,1,0:T(8,128)(2,1)S(1)}, bf16[1,1,256,512]{3,2,1,0:T(8,128)(2,1)S(1)}, u32[]{:S(2)}, u32[]{:S(2)}) collective-permute-start(bf16[1,1,256,512]{3,2,1,0:T(8,128)(2,1)S(1)} %add_convert_fusion.4), channel_id=1, source_target_pairs={{0,256},{64,320},{128,384},{192,448},{256,0},{320,64},{384,128},{4... | collective-permute-start | bytes 786440 | tf_op jit(solution)/shard_map/ppermute | solution.py:88
  177.2 21.5 %collective-permute-start.13 = (bf16[256,512]{1,0:T(8,128)(2,1)S(1)}, bf16[256,512]{1,0:T(8,128)(2,1)S(1)}, u32[]{:S(2)}, u32[]{:S(2)}) collective-permute-start(bf16[256,512]{1,0:T(8,128)(2,1)S(1)} %fusion.29), channel_id=1, source_target_pairs={{0,0},{4,128},{8,256},{12,384},{64,64},{68,192},{72,320},{76,448},... | collective-permute-start | bytes 786440 | tf_op jit(solution)/shard_map/ppermute | solution.py:109
